TPU v7x, 32 devices: a whole 2x2x4 slice. The times are simulated.
32 devices in a mesh: dp: 4 (over x, core), context: 2 (over y), experts: 4 (over z).
Axes of the slice: x: 2, y: 2, z: 4, core: 2. Of those that a mesh axis runs over, the one named last changes fastest.
Arguments:
- activations: bfloat16 [2, 16, 256, 1024], P(None, ('dp', 'experts'), 'context'), may hold values from -6 to 6
- cotangent: bfloat16 [2, 16, 256, 1024], P(None, ('dp', 'experts'), 'context'), may hold values from -6 to 6
- dealing: int32 [2, 16, 256], P(None, ('dp', 'experts')), may hold values from 0 to 255, each once within a row
- lengths: int32 [2, 16], P(None, ('dp', 'experts')), may hold values from 128 to 256, as said below
- routes: int32 [2, 16, 256, 2], P(None, ('dp', 'experts'), 'context'), may hold values from 0 to 3, all different within a row
- buckets: int32 [256], replicated, may hold values from 0 to 31, as said below
- w_query: bfloat16 [1024, 1024], P(('dp', 'context', 'experts')), may hold values from -0.1875 to 0.1875
- w_key: bfloat16 [1024, 1024], P(('dp', 'context', 'experts')), may hold values from -0.1875 to 0.1875
- w_value: bfloat16 [1024, 1024], P(('dp', 'context', 'experts')), may hold values from -0.1875 to 0.1875
- w_out: bfloat16 [1024, 1024], P(('dp', 'context', 'experts')), may hold values from -1.5 to 1.5
- w_router: bfloat16 [1024, 4], P(('dp', 'context', 'experts')), may hold values from -0.125 to 0.125
- norm_first: bfloat16 [1024], P(('dp', 'context', 'experts')), may hold values from 0.099609375 to 1.8984375
- norm_second: bfloat16 [1024], P(('dp', 'context', 'experts')), may hold values from 0.099609375 to 1.8984375
- bias_table: bfloat16 [32, 16], replicated, may hold values from -4 to 4
- w_gate: bfloat16 [4, 1024, 2816], P('experts', ('dp', 'context')), may hold values from -0.1875 to 0.1875
- w_up: bfloat16 [4, 1024, 2816], P('experts', ('dp', 'context')), may hold values from -0.1875 to 0.1875
- w_down: bfloat16 [4, 2816, 1024], P('experts', ('dp', 'context')), may hold values from -0.15625 to 0.15625
Outputs:
- output: bfloat16 [2, 16, 256, 1024], P(None, ('dp', 'experts'), 'context')
- grad_input: bfloat16 [2, 16, 256, 1024], P(None, ('dp', 'experts'), 'context')
- grad_query: float32 [1024, 1024], P(('dp', 'context', 'experts'))
- grad_key: float32 [1024, 1024], P(('dp', 'context', 'experts'))
- grad_value: float32 [1024, 1024], P(('dp', 'context', 'experts'))
- grad_out: float32 [1024, 1024], P(('dp', 'context', 'experts'))
- grad_router: float32 [1024, 4], P(('dp', 'context', 'experts'))
- grad_first: float32 [1024], P(('dp', 'context', 'experts'))
- grad_second: float32 [1024], P(('dp', 'context', 'experts'))
- grad_table: float32 [32, 16], replicated
- grad_gate: float32 [4, 1024, 2816], P('experts', ('dp', 'context'))
- grad_up: float32 [4, 1024, 2816], P('experts', ('dp', 'context'))
- grad_down: float32 [4, 2816, 1024], P('experts', ('dp', 'context'))
Inputs may be any that keep to these rules, and one draw needn't show every extreme that they name: `dealing`: each row is a permutation. `lengths`: some sequence has length 256. `routes`: the two experts of a slot differ. `buckets`: non-decreasing in the offset; an offset o below 16 has bucket o; offset 256 - 1 has bucket 32 - 1.
All inputs are finite; a program needn't handle non-finite values.
Results may differ from a plain program's by a relative error of at most 0.015.
Values may be sent and summed in bfloat16 or wider, within the bound.
A program may use at most 512 MiB of HBM per device.

v0:
```python
import functools

import jax
import jax.numpy as jnp
from jax import lax
from jax.experimental import pallas as pl
from jax.experimental.pallas import tpu as pltpu
from jax.sharding import PartitionSpec as P

epsilon = 1e-06
masked_score = -1e30
ALL = ("dp", "context", "experts")
F32 = jnp.float32
BF16 = jnp.bfloat16


def dot_f32(spec, left, right):
    return jnp.einsum(spec, left, right, preferred_element_type=F32)


def swap(value, axis, offset):
    size = lax.axis_size(axis)
    return lax.ppermute(value, axis, [(i, i ^ offset) for i in range(size)])


def reorder(pieces, index):
    pieces = list(pieces)
    bit = 1
    while bit < len(pieces):
        flag = (index // bit) % 2 == 1
        pieces = [jnp.where(flag, pieces[j ^ bit], pieces[j]) for j in range(len(pieces))]
        bit *= 2
    return pieces


def reorder_lanes(value, blocks, index):
    return jnp.concatenate(reorder(jnp.split(value, blocks, axis=-1), index), axis=-1)


def toeplitz_bias(line, size):
    rows = jnp.broadcast_to(line, (size, 2 * size))
    return pltpu.roll(rows, 0, 1, stride=1, stride_axis=0)[:, :size]


def masked_scores(query, key, line, length, scale):
    size = query.shape[0]
    scores = lax.dot_general(query, key, (((1,), (1,)), ((), ())), preferred_element_type=F32)
    scores = scores * scale + toeplitz_bias(line, size)
    row_id = lax.broadcasted_iota(jnp.int32, (size, size), 0)
    col_id = lax.broadcasted_iota(jnp.int32, (size, size), 1)
    allowed = (row_id >= col_id) & (col_id < length)
    return jnp.where(allowed, scores, masked_score)


def soft(scores):
    top_score = jnp.max(scores, axis=-1, keepdims=True)
    raised = jnp.exp(scores - top_score)
    return raised / jnp.sum(raised, axis=-1, keepdims=True)


def attend_kernel(heads, head_size, length_ref, line_ref, qkv_ref, mixed_ref):
    scale = head_size ** (-0.5)
    width = heads * head_size
    length = length_ref[pl.program_id(0)]
    for head in range(heads):
        query = qkv_ref[0, :, head * head_size : (head + 1) * head_size]
        key = qkv_ref[0, :, width + head * head_size : width + (head + 1) * head_size]
        value = qkv_ref[0, :, 2 * width + head * head_size : 2 * width + (head + 1) * head_size]
        scores = masked_scores(query, key, line_ref[head : head + 1, :], length, scale)
        probs = soft(scores).astype(BF16)
        mixed = jnp.dot(probs, value, preferred_element_type=F32)
        mixed_ref[0, :, head * head_size : (head + 1) * head_size] = mixed.astype(BF16)


def attend(qkv, lines, lengths, heads):
    micro, seq, width = qkv.shape
    width = width // 3
    head_size = width // heads
    return pl.pallas_call(
        functools.partial(attend_kernel, heads, head_size),
        grid=(micro,),
        out_shape=jax.ShapeDtypeStruct((micro, seq, width), BF16),
        in_specs=[
            pl.BlockSpec(memory_space=pltpu.SMEM),
            pl.BlockSpec(lines.shape, lambda i: (0, 0)),
            pl.BlockSpec((1, seq, 3 * width), lambda i: (i, 0, 0)),
        ],
        out_specs=pl.BlockSpec((1, seq, width), lambda i: (i, 0, 0)),
        compiler_params=pltpu.CompilerParams(vmem_limit_bytes=32 * 2**20),
    )(lengths, lines, qkv)


def diagonal_sums(grad):
    size = grad.shape[0]
    wide = jnp.concatenate([grad, jnp.zeros_like(grad)], axis=1)
    rows = size
    while rows > 1:
        rows //= 2
        lower = pltpu.roll(wide[rows:], 2 * size - rows, 1)
        wide = wide[:rows] + lower
    return wide


def attend_back_kernel(
    heads, head_size, length_ref, line_ref, qkv_ref, grad_ref, out_ref, diag_ref
):
    scale = head_size ** (-0.5)
    width = heads * head_size
    length = length_ref[pl.program_id(0)]

    @pl.when(pl.program_id(0) == 0)
    def _():
        diag_ref[...] = jnp.zeros_like(diag_ref)

    for head in range(heads):
        at = [
            slice(part * width + head * head_size, part * width + (head + 1) * head_size)
            for part in range(3)
        ]
        query, key, value = (qkv_ref[0, :, part] for part in at)
        grad = grad_ref[0, :, at[0]]
        scores = masked_scores(query, key, line_ref[head : head + 1, :], length, scale)
        probs = soft(scores)
        prob_grad = lax.dot_general(
            grad, value, (((1,), (1,)), ((), ())), preferred_element_type=F32
        )
        delta = jnp.sum(probs * prob_grad, axis=-1, keepdims=True)
        score_grad = (probs * (prob_grad - delta)).astype(BF16)
        diag_ref[head : head + 1, :] += diagonal_sums(score_grad.astype(F32))
        query_grad = jnp.dot(score_grad, key, preferred_element_type=F32) * scale
        key_grad = (
            lax.dot_general(
                score_grad, query, (((0,), (0,)), ((), ())), preferred_element_type=F32
            )
            * scale
        )
        value_grad = lax.dot_general(
            probs.astype(BF16), grad, (((0,), (0,)), ((), ())), preferred_element_type=F32
        )
        out_ref[0, :, at[0]] = query_grad.astype(BF16)
        out_ref[0, :, at[1]] = key_grad.astype(BF16)
        out_ref[0, :, at[2]] = value_grad.astype(BF16)


def attend_back(qkv, grad, lines, lengths, heads):
    micro, seq, width = grad.shape
    head_size = width // heads
    return pl.pallas_call(
        functools.partial(attend_back_kernel, heads, head_size),
        grid=(micro,),
        out_shape=(
            jax.ShapeDtypeStruct(qkv.shape, BF16),
            jax.ShapeDtypeStruct(lines.shape, F32),
        ),
        in_specs=[
            pl.BlockSpec(memory_space=pltpu.SMEM),
            pl.BlockSpec(lines.shape, lambda i: (0, 0)),
            pl.BlockSpec((1, seq, 3 * width), lambda i: (i, 0, 0)),
            pl.BlockSpec((1, seq, width), lambda i: (i, 0, 0)),
        ],
        out_specs=(
            pl.BlockSpec((1, seq, 3 * width), lambda i: (i, 0, 0)),
            pl.BlockSpec(lines.shape, lambda i: (0, 0)),
        ),
        compiler_params=pltpu.CompilerParams(vmem_limit_bytes=32 * 2**20),
    )(lengths, lines, qkv, grad)


def halve(value, axis, bit, flag):
    kept = jnp.where(flag, value[1], value[0])
    sent = jnp.where(flag, value[0], value[1]).astype(BF16)
    return kept + swap(sent, axis, bit).astype(F32)


def scatter_sum(value, dp_index, expert_index):
    dp_count, ctx_count, expert_count = value.shape[:3]
    rest = value.shape[3:]
    count, bit = dp_count, 1
    while count > 1:
        shaped = value.reshape((count // 2, 2, -1))
        value = halve(jnp.moveaxis(shaped, 1, 0), "dp", bit, (dp_index // bit) % 2 == 1)
        count //= 2
        bit *= 2
    value = value.reshape((ctx_count, expert_count) + rest)
    count, bit = expert_count, 1
    while count > 1:
        shaped = value.reshape((ctx_count, count // 2, 2) + rest)
        value = halve(jnp.moveaxis(shaped, 2, 0), "experts", bit, (expert_index // bit) % 2 == 1)
        count //= 2
        bit *= 2
    return value.reshape((ctx_count,) + rest)


def norm_pull(features, inverse, gain, grad):
    lifted = gain * grad
    mean_part = jnp.mean(lifted * features, axis=-1, keepdims=True)
    back = inverse * lifted - features * (inverse * inverse * inverse) * mean_part
    gain_grad = jnp.sum(grad * features * inverse, axis=(0, 1))
    return back, gain_grad


def gelu_parts(pre):
    root = 0.7978845608028654
    cubic = 0.044715
    square = pre * pre
    wave = jnp.tanh(root * (pre + cubic * pre * square))
    value = 0.5 * pre * (1.0 + wave)
    slope = 0.5 * (1.0 + wave) + 0.5 * pre * (1.0 - wave * wave) * root * (
        1.0 + 3.0 * cubic * square
    )
    return value, slope


def down_routes(dp_count, ctx_count, expert_count, core, ctx_offset):
    pairs = []
    for dp in range(dp_count):
        for ctx in range(ctx_count):
            for expert in range(expert_count):
                high, low = dp // 2, dp % 2
                to_high = high if low == core else high ^ 1
                target = ((to_high * 2 + high) * ctx_count + (ctx ^ ctx_offset)) * expert_count
                pairs.append(((dp * ctx_count + ctx) * expert_count + expert, target + expert))
    return pairs


def body(
    activations,
    cotangent,
    dealing,
    lengths,
    routes,
    buckets,
    w_query,
    w_key,
    w_value,
    w_out,
    w_router,
    norm_first,
    norm_second,
    bias_table,
    w_gate,
    w_up,
    w_down,
):
    micro, _, rows_dev, width = activations.shape
    seq = dealing.shape[2]
    bucket_count, head_count = bias_table.shape
    dp_count, ctx_count, expert_count = (lax.axis_size(name) for name in ALL)
    dp_index, ctx_index, expert_index = (lax.axis_index(name) for name in ALL)
    high, low = dp_index // 2, dp_index % 2
    heads = head_count // ctx_count
    head_size = width // head_count
    own_width = heads * head_size
    experts = w_router.shape[1]
    top_count = routes.shape[3]
    capacity = (5 * rows_dev * top_count + 4 * experts - 1) // (4 * experts)
    slots = -(-capacity // 16) * 16
    ff = w_gate.shape[2]
    half_ff = ff // 2
    weight_rows = w_query.shape[0]
    plane = dp_count * ctx_count
    plane_index = dp_index * ctx_count + ctx_index
    act = activations[:, 0]
    cot = cotangent[:, 0]
    deal = dealing[:, 0]
    length = lengths[:, 0]
    route = routes[:, 0]

    extras = jnp.concatenate(
        [w_router, norm_first[:, None], norm_second[:, None]], axis=1
    )
    extras = jnp.pad(extras, ((0, 0), (0, 128 - extras.shape[1])))
    column_parts = [
        jnp.split(weight, ctx_count, axis=1) for weight in (w_query, w_key, w_value)
    ]
    packs = [
        jnp.concatenate([part[c] for part in column_parts] + [extras], axis=1)
        for c in range(ctx_count)
    ]
    packs = reorder(packs, ctx_index)
    packs = [packs[0]] + [swap(packs[k], "context", k) for k in range(1, ctx_count)]
    packs = jnp.stack(reorder(packs, ctx_index))
    dense = lax.all_gather(packs, ("dp", "experts"), axis=0, tiled=False)
    dense = dense.reshape((dp_count, expert_count) + packs.shape)
    dense = jnp.transpose(dense, (0, 2, 1, 3, 4)).reshape(width, -1)
    qkv_w = dense[:, : 3 * own_width]
    router_w = dense[:, 3 * own_width : 3 * own_width + experts]
    gain_one = dense[:, 3 * own_width + experts].astype(F32)
    gain_two = dense[:, 3 * own_width + experts + 1].astype(F32)
    out_w = lax.all_gather(w_out, ALL, axis=0, tiled=True)

    gate_up = [
        jnp.concatenate([w_gate[0, :, h * half_ff : (h + 1) * half_ff], w_up[0, :, h * half_ff : (h + 1) * half_ff]], axis=1)
        for h in range(2)
    ]
    halves = reorder(gate_up, low)
    gate_blocks = []
    for j in range(plane):
        dp_offset, ctx_offset = j // ctx_count, j % ctx_count
        piece = halves[dp_offset % 2]
        if dp_offset:
            piece = swap(piece, "dp", dp_offset)
        if ctx_offset:
            piece = swap(piece, "context", ctx_offset) if not dp_offset else piece
        gate_blocks.append(piece)
    for j in range(plane):
        dp_offset, ctx_offset = j // ctx_count, j % ctx_count
        if dp_offset and ctx_offset:
            gate_blocks[j] = swap(gate_blocks[dp_offset * ctx_count], "context", ctx_offset)
    gate_up_w = jnp.concatenate(gate_blocks, axis=0)
    down_w = jnp.zeros((half_ff, width), BF16)
    down_rows = w_down.shape[1]
    for ctx_offset in range(ctx_count):
        for core in range(2):
            pairs = down_routes(dp_count, ctx_count, expert_count, core, ctx_offset)
            piece = lax.ppermute(w_down[0], ALL, pairs)
            from_core = jnp.where(low == high, core, 1 - core)
            place = (from_core * ctx_count + (ctx_index ^ ctx_offset)) * down_rows
            down_w = lax.dynamic_update_slice(down_w, piece, (place, 0))

    act_all = jnp.concatenate(
        reorder([act] + [swap(act, "context", k) for k in range(1, ctx_count)], ctx_index), axis=1
    )
    cot_all = jnp.concatenate(
        reorder([cot] + [swap(cot, "context", k) for k in range(1, ctx_count)], ctx_index), axis=1
    )
    position_ids = jnp.arange(seq, dtype=jnp.int32)
    slot_blocks = [
        lax.dynamic_slice_in_dim(deal, (ctx_index ^ k) * rows_dev, rows_dev, axis=1)
        for k in range(ctx_count)
    ]
    hot = [
        (block[:, :, None] == position_ids[None, None, :]).astype(BF16) for block in slot_blocks
    ]
    my_positions = ctx_index * rows_dev + jnp.arange(rows_dev, dtype=jnp.int32)
    hot_mine = [
        (block[:, :, None] == my_positions[None, None, :]).astype(BF16) for block in slot_blocks
    ]
    live = slot_blocks[0] < length[:, None]
    live_rows = live.astype(F32)[:, :, None]
    bucket_hot = (buckets[:, None] == jnp.arange(bucket_count)[None, :]).astype(BF16)
    own_table = lax.dynamic_slice_in_dim(bias_table, ctx_index * heads, heads, axis=1)
    lookup = dot_f32("sb,bh->hs", bucket_hot, own_table)
    lines = jnp.concatenate(
        [lookup[:, :1], jnp.zeros((heads, seq), F32), lookup[:, :0:-1]], axis=1
    )

    rows_all = act_all.astype(F32)
    inverse_one = lax.rsqrt(jnp.mean(rows_all * rows_all, axis=-1, keepdims=True) + epsilon)
    normed = (rows_all * inverse_one * gain_one).astype(BF16)
    qkv = dot_f32("mpd,dw->mpw", normed, qkv_w).astype(BF16)
    mixed_own = attend(qkv, lines, length, heads)
    mixed_parts = [
        dot_f32("msp,mpw->msw", hot[k], mixed_own).astype(BF16) for k in range(ctx_count)
    ]
    mixed_parts = [mixed_parts[0]] + [
        swap(mixed_parts[k], "context", k) for k in range(1, ctx_count)
    ]
    mixed = jnp.concatenate(reorder(mixed_parts, ctx_index), axis=-1)

    rows_in = dot_f32("msp,mpd->msd", hot[0], act_all)
    cot_rows = dot_f32("msp,mpd->msd", hot[0], cot_all)
    branch = dot_f32("msi,io->mso", mixed, out_w)
    hidden = rows_in + branch * live_rows
    inverse_two = lax.rsqrt(jnp.mean(hidden * hidden, axis=-1, keepdims=True) + epsilon)
    normed_two = (hidden * inverse_two * gain_two).astype(BF16)
    logits = dot_f32("msd,de->mse", normed_two, router_w)
    route_hot = (route[..., None] == jnp.arange(experts)).astype(F32)
    chosen = jnp.sum(route_hot * logits[:, :, None, :], axis=3)
    gate_probs = jax.nn.softmax(chosen, axis=-1)

    flat_hot = (route_hot * live_rows[..., None]).reshape(micro, rows_dev * top_count, experts)
    pair_ids = jnp.arange(rows_dev * top_count)
    before = (pair_ids[:, None] > pair_ids[None, :]).astype(BF16)
    earlier = dot_f32("ab,mbe->mae", before, flat_hot.astype(BF16))
    rank = jnp.sum(earlier * flat_hot, axis=2).astype(jnp.int32).reshape(route.shape)
    kept = live[:, :, None] & (rank < capacity)
    target = jnp.where(kept, (route ^ expert_index) * slots + rank, -1)
    place_ids = jnp.arange(experts * slots, dtype=jnp.int32)
    pick = [
        (target[:, None, :, j] == place_ids[None, :, None]) for j in range(top_count)
    ]
    pick_any = functools.reduce(jnp.logical_or, pick).astype(BF16)
    pick_bf = [p.astype(BF16) for p in pick]
    prob_rows = sum(
        jnp.sum(jnp.where(pick[j], gate_probs[:, None, :, j], 0.0), axis=2)
        for j in range(top_count)
    )

    def by_expert(value):
        shaped = value.reshape((micro, experts, slots) + value.shape[2:])
        return jnp.moveaxis(shaped, 1, 0)

    def exchange(value):
        parts = [value[0]] + [swap(value[k], "experts", k) for k in range(1, expert_count)]
        return jnp.stack(parts)

    normed_rel = reorder_lanes(normed_two, plane, plane_index)
    sent_rows = by_expert(dot_f32("mrs,msd->mrd", pick_any, normed_rel).astype(BF16))
    sent_up = by_expert(
        dot_f32("mrs,msd->mrd", pick_any, cot_rows.astype(BF16)).astype(BF16)
    )
    row_count = expert_count * micro * slots
    own_x = exchange(sent_rows).reshape(row_count, width)
    own_u = exchange(sent_up).reshape(row_count, width)
    own_p = exchange(by_expert(prob_rows)).reshape(row_count, 1)
    own_g = (own_p * own_u.astype(F32)).astype(BF16)

    def core_swap(value):
        blocks = jnp.split(value, plane, axis=-1)
        return jnp.concatenate([blocks[j ^ ctx_count] for j in range(plane)], axis=-1)

    all_x = jnp.concatenate([own_x, core_swap(swap(own_x, "dp", 1))], axis=0)
    all_g = jnp.concatenate([own_g, swap(own_g, "dp", 1)], axis=0)

    pre_up = dot_f32("rd,df->rf", all_x, gate_up_w)
    gelu_value, gelu_slope = gelu_parts(pre_up[:, :half_ff])
    up_part = pre_up[:, half_ff:]
    activated = (gelu_value * up_part).astype(BF16)
    act_grad = dot_f32("rd,fd->rf", all_g, down_w)
    pre_grad = (act_grad * up_part * gelu_slope).astype(BF16)
    up_grad = (act_grad * gelu_value).astype(BF16)
    both_grad = jnp.concatenate([pre_grad, up_grad], axis=1)
    back_part = dot_f32("rf,df->rd", both_grad, gate_up_w)
    out_part = dot_f32("rf,fd->rd", activated, down_w)
    out_own = (
        out_part[:row_count] + swap(out_part[row_count:].astype(BF16), "dp", 1).astype(F32)
    ).astype(BF16)
    back_own = (
        back_part[:row_count]
        + swap(core_swap(back_part[row_count:].astype(BF16)), "dp", 1).astype(F32)
    ).astype(BF16)
    gate_rows = jnp.sum(own_u.astype(F32) * out_own.astype(F32), axis=-1)

    def to_source(value):
        parts = value.reshape((expert_count, micro, slots) + value.shape[1:])
        parts = exchange(parts)
        return jnp.moveaxis(parts, 0, 1).reshape((micro, experts * slots) + value.shape[1:])

    back_rows = to_source(back_own)
    gate_back = to_source(gate_rows)
    out_rows = to_source(out_own)

    gate_up_total = dot_f32("rd,rf->df", all_x, both_grad)
    down_total = dot_f32("rf,rd->fd", activated, all_g)

    gate_up_sums = [0.0, 0.0]
    for j in range(plane):
        dp_offset, ctx_offset = j // ctx_count, j % ctx_count
        block = gate_up_total[j * (width // plane) : (j + 1) * (width // plane)].astype(BF16)
        pairs = [
            (
                (d * ctx_count + c) * expert_count + e,
                ((d ^ dp_offset) * ctx_count + (c ^ ctx_offset)) * expert_count + e,
            )
            for d in range(dp_count)
            for c in range(ctx_count)
            for e in range(expert_count)
        ]
        if j:
            block = lax.ppermute(block, ALL, pairs)
        gate_up_sums[dp_offset % 2] = gate_up_sums[dp_offset % 2] + block.astype(F32)
    first_half, second_half = reorder(gate_up_sums, low)
    grad_gate = jnp.concatenate([first_half[:, :half_ff], second_half[:, :half_ff]], axis=1)
    grad_up = jnp.concatenate([first_half[:, half_ff:], second_half[:, half_ff:]], axis=1)
    grad_down = 0.0
    for ctx_offset in range(ctx_count):
        for core in range(2):
            pairs = down_routes(dp_count, ctx_count, expert_count, core, ctx_offset)
            from_core = jnp.where(low == high, core, 1 - core)
            place = (from_core * ctx_count + (ctx_index ^ ctx_offset)) * down_rows
            piece = lax.dynamic_slice_in_dim(down_total, place, down_rows, axis=0).astype(BF16)
            arrived = lax.ppermute(piece, ALL, [(b, a) for a, b in pairs])
            grad_down = grad_down + arrived.astype(F32)

    pair_out = [dot_f32("mrs,mrd->msd", pick_bf[j], out_rows) for j in range(top_count)]
    final = hidden + sum(gate_probs[:, :, j, None] * pair_out[j] for j in range(top_count))
    final = final.astype(BF16)
    gate_grad = jnp.stack(
        [
            jnp.sum(jnp.where(pick[j], gate_back[:, :, None], 0.0), axis=1)
            for j in range(top_count)
        ],
        axis=-1,
    )
    chosen_grad = gate_probs * (
        gate_grad - jnp.sum(gate_probs * gate_grad, axis=-1, keepdims=True)
    )
    logit_grad = jnp.sum(route_hot * chosen_grad[..., None], axis=2).astype(BF16)
    normed_grad = reorder_lanes(
        dot_f32("mrs,mrd->msd", pick_any, back_rows), plane, plane_index
    ) + dot_f32("mse,de->msd", logit_grad, router_w)
    router_total = dot_f32("msd,mse->de", normed_two, logit_grad)
    hidden_norm_grad, second_total = norm_pull(hidden, inverse_two, gain_two, normed_grad)
    hidden_grad = cot_rows + hidden_norm_grad
    branch_grad = (hidden_grad * live_rows).astype(BF16)
    hidden_low = hidden_grad.astype(BF16)
    out_total = dot_f32("msi,mso->io", mixed, branch_grad)
    mixed_grad = dot_f32("mso,io->msi", branch_grad, out_w).astype(BF16)
    grad_parts = reorder(jnp.split(mixed_grad, ctx_count, axis=-1), ctx_index)
    grad_parts = [grad_parts[0]] + [
        swap(grad_parts[k], "context", k) for k in range(1, ctx_count)
    ]
    mixed_back = sum(
        dot_f32("msp,msw->mpw", hot[k], grad_parts[k]) for k in range(ctx_count)
    ).astype(BF16)
    qkv_grad, diagonals = attend_back(qkv, mixed_back, lines, length, heads)
    qkv_total = dot_f32("mpd,mpw->dw", normed, qkv_grad)
    first_part = dot_f32("mpw,dw->mpd", qkv_grad, qkv_w)
    first_total = jnp.sum(first_part * rows_all * inverse_one, axis=(0, 1))
    blocks = [
        lax.dynamic_slice_in_dim(first_part, (ctx_index ^ k) * rows_dev, rows_dev, axis=1)
        for k in range(ctx_count)
    ]
    first_grad = blocks[0] + sum(
        swap(blocks[k].astype(BF16), "context", k).astype(F32) for k in range(1, ctx_count)
    )

    def to_positions(value):
        parts = [value] + [swap(value, "context", k) for k in range(1, ctx_count)]
        return sum(dot_f32("msp,msd->mpd", hot_mine[k], parts[k]) for k in range(ctx_count))

    rows_mine = act.astype(F32)
    inverse_mine = lax.rsqrt(jnp.mean(rows_mine * rows_mine, axis=-1, keepdims=True) + epsilon)
    rows_back, _ = norm_pull(rows_mine, inverse_mine, gain_one, first_grad)
    grad_input = (to_positions(hidden_low) + rows_back).astype(BF16)[:, None]
    output = to_positions(final).astype(BF16)[:, None]

    owners = (dp_count, ctx_count, expert_count, weight_rows)
    out_pack = jnp.concatenate(
        [out_total, router_total, second_total[:, None]], axis=1
    )
    out_pack = jnp.pad(out_pack, ((0, 0), (0, width + 128 - out_pack.shape[1])))
    out_pack = scatter_sum(out_pack.reshape(owners + (-1,)), dp_index, expert_index)
    qkv_pack = jnp.pad(
        jnp.concatenate([qkv_total, first_total[:, None]], axis=1), ((0, 0), (0, 127))
    )
    qkv_pack = scatter_sum(qkv_pack.reshape(owners + (-1,)), dp_index, expert_index)

    def across(value):
        parts = reorder([value[c] for c in range(ctx_count)], ctx_index)
        return [parts[0]] + [
            swap(parts[k].astype(BF16), "context", k).astype(F32) for k in range(1, ctx_count)
        ]

    out_sum = sum(across(out_pack))
    qkv_parts = across(qkv_pack)
    grad_first = sum(part[:, 3 * own_width] for part in qkv_parts)
    qkv_parts = reorder(qkv_parts, ctx_index)
    grad_query, grad_key, grad_value = (
        jnp.concatenate(
            [part[:, i * own_width : (i + 1) * own_width] for part in qkv_parts], axis=1
        )
        for i in range(3)
    )
    grad_out = out_sum[:, :width]
    grad_router = out_sum[:, width : width + experts]
    grad_second = out_sum[:, width + experts]
    offsets = jnp.concatenate([diagonals[:, :1], diagonals[:, : seq : -1]], axis=1)
    table_part = jnp.einsum(
        "hs,sb->bh", offsets, bucket_hot.astype(F32), precision=lax.Precision.HIGHEST
    )
    table_full = lax.dynamic_update_slice(
        jnp.zeros(bias_table.shape, F32), table_part, (0, ctx_index * heads)
    )
    grad_table = lax.psum(table_full, ALL)
    return (
        output,
        grad_input,
        grad_query,
        grad_key,
        grad_value,
        grad_out,
        grad_router,
        grad_first,
        grad_second,
        grad_table,
        grad_gate[None],
        grad_up[None],
        grad_down[None],
    )


def solution(mesh):
    tokens = P(None, ("dp", "experts"), "context", None)
    sequences = P(None, ("dp", "experts"))
    rows = P(("dp", "context", "experts"), None)
    gains = P(("dp", "context", "experts"))
    experts = P("experts", ("dp", "context"), None)
    placed = (
        (tokens, tokens, P(None, ("dp", "experts"), None), sequences, tokens, P())
        + (rows,) * 5
        + (gains, gains, P())
        + (experts,) * 3
    )
    return jax.shard_map(
        body,
        mesh=mesh,
        in_specs=placed,
        out_specs=(tokens, tokens) + (rows,) * 5 + (gains, gains, P()) + (experts,) * 3,
        check_vma=False,
    )
```

profile of v0, /device:TPU:0, one launch (start us, length us, event | category | flops | bytes accessed | tf_op | source)
XLA Modules:
  0.0 749.2 jit_solution(301563122992894643)
XLA Ops:
  36.0 34.4 %collective-permute-done.23 = bf16[2,128,1024]{2,1,0:T(8,128)(2,1)} collective-permute-done((bf16[2,128,1024]{2,1,0:T(8,128)(2,1)}, bf16[2,128,1024]{2,1,0:T(8,128)(2,1)}, u32[]{:S(2)}, u32[]{:S(2)}) %collective-permute-start.23) | collective-permute-done | bytes 524320 | tf_op jit(solution)/shard_map/ppermute | solution.py:23
  76.0 9.1 %collective-permute-done = bf16[2,128,1024]{2,1,0:T(8,128)(2,1)S(1)} collective-permute-done((bf16[2,128,1024]{2,1,0:T(8,128)(2,1)S(1)}, bf16[2,128,1024]{2,1,0:T(8,128)(2,1)S(1)}, u32[]{:S(2)}, u32[]{:S(2)}) %collective-permute-start) | collective-permute-done | bytes 524320 | tf_op jit(solution)/shard_map/ppermute | solution.py:23
  96.1 10.1 %collective-permute-done.10 = bf16[128,2816]{1,0:T(8,128)(2,1)} collective-permute-done((bf16[128,2816]{1,0:T(8,128)(2,1)S(1)}, bf16[128,2816]{1,0:T(8,128)(2,1)}, u32[]{:S(2)}, u32[]{:S(2)}) %collective-permute-start.10) | collective-permute-done | bytes 720928 | tf_op jit(solution)/shard_map/ppermute | solution.py:23
  131.7 17.0 %collective-permute-done.2 = bf16[2,128,512]{2,1,0:T(8,128)(2,1)S(1)} collective-permute-done((bf16[2,128,512]{2,1,0:T(8,128)(2,1)S(1)}, bf16[2,128,512]{2,1,0:T(8,128)(2,1)S(1)}, u32[]{:S(2)}, u32[]{:S(2)}) %collective-permute-start.2) | collective-permute-done | bytes 262176 | tf_op jit(solution)/shard_map/ppermute | solution.py:23
  163.2 9.5 %collective-permute-done.3 = bf16[2,80,1024]{2,1,0:T(8,128)(2,1)S(1)} collective-permute-done((bf16[2,80,1024]{2,1,0:T(8,128)(2,1)S(1)}, bf16[2,80,1024]{2,1,0:T(8,128)(2,1)S(1)}, u32[]{:S(2)}, u32[]{:S(2)}) %collective-permute-start.3) | collective-permute-done | bytes 327712 | tf_op jit(solution)/shard_map/ppermute | solution.py:23
  173.8 9.5 %collective-permute-done.4 = bf16[2,80,1024]{2,1,0:T(8,128)(2,1)S(1)} collective-permute-done((bf16[2,80,1024]{2,1,0:T(8,128)(2,1)S(1)}, bf16[2,80,1024]{2,1,0:T(8,128)(2,1)S(1)}, u32[]{:S(2)}, u32[]{:S(2)}) %collective-permute-start.4) | collective-permute-done | bytes 327712 | tf_op jit(solution)/shard_map/ppermute | solution.py:23
  196.8 10.3 %fusion.140 = f32[1280,2816]{1,0:T(8,128)S(1)} fusion(bf16[1024,2816]{1,0:T(8,128)(2,1)} %constant_dynamic-update-slice_fusion, bf16[640,256]{1,0:T(8,128)(2,1)S(1)} %get-tuple-element.157, bf16[640,256]{1,0:T(8,128)(2,1)S(1)} %get-tuple-element.158, bf16[640,256]{1,0:T(8,128)(2,1)S(1)} %get-tuple-element.159, ...), kind=kOutput, calls=%fused_computation.357 | convolution fusion | flops 7395082240 | bytes 22806528 | tf_op jit(solution)/shard_map/rd,df->rf/dot_general | solution.py:18
  230.4 18.5 %collective-permute-start.35 = (f32[2,80]{1,0:T(2,128)}, f32[2,80]{1,0:T(2,128)}, u32[]{:S(2)}, u32[]{:S(2)}) collective-permute-start(f32[2,80]{1,0:T(2,128)} %squeeze.149), channel_id=1, source_target_pairs={{0,1},{1,0},{2,3},{3,2},{4,5},{5,4},{6,7},{7,6},{8,9},{9,8},{10,11... | collective-permute-start | bytes 1928 | tf_op jit(solution)/shard_map/ppermute | solution.py:23
  286.3 9.7 %collective-permute-done.22 = bf16[2,128,1024]{2,1,0:T(8,128)(2,1)S(1)} collective-permute-done((bf16[2,128,1024]{2,1,0:T(8,128)(2,1)S(1)}, bf16[2,128,1024]{2,1,0:T(8,128)(2,1)S(1)}, u32[]{:S(2)}, u32[]{:S(2)}) %collective-permute-start.22) | collective-permute-done | bytes 524320 | tf_op jit(solution)/shard_map/ppermute | solution.py:23
  297.2 15.6 %multiply_convert_fusion.1 = (bf16[1280,1408]{1,0:T(8,128)(2,1)}, bf16[1280,1408]{1,0:T(8,128)(2,1)}) fusion(f32[1280,2816]{1,0:T(8,128)} %copy-done.5, bf16[1408,1024]{1,0:T(8,128)(2,1)} %constant_dynamic-update-slice_fusion.8, bf16[640,1024]{1,0:T(8,128)(2,1)S(1)} %collective-permute-done.30, bf16[640,1024]{1,0:T(8,128)(2,1)S(1)} %fusion.2), kind=kOutput, calls=%fused_computation.3 | convolution fusion | flops 3735879680 | bytes 27131904 | tf_op jit(solution)/shard_map/rd,fd->rf/dot_general | solution.py:18
  312.8 10.9 %convolution_convert_fusion = bf16[1024,2816]{1,0:T(8,128)(2,1)S(1)} fusion(bf16[1280,1408]{1,0:T(8,128)(2,1)} %get-tuple-element.125, bf16[1280,1408]{1,0:T(8,128)(2,1)} %get-tuple-element.124, bf16[640,256]{1,0:T(8,128)(2,1)S(1)} %copy-done.38, bf16[640,256]{1,0:T(8,128)(2,1)S(1)} %copy-done.40, bf16[640,256]{1,0:T(8,128)(2,1)S(1)} %copy-done.42, ...), kind=kOutput, calls=%fused_computation.10 | convolution fusion | flops 7412383744 | bytes 15597568 | tf_op jit(solution)/shard_map/rd,rf->df/dot_general | solution.py:18
  327.5 13.2 %fusion.162 = (bf16[1280,1024]{1,0:T(8,128)(2,1)}, f32[1280,1024]{1,0:T(8,128)}) fusion(bf16[1024,2816]{1,0:T(8,128)(2,1)} %constant_dynamic-update-slice_fusion, bf16[1280,1408]{1,0:T(8,128)(2,1)} %get-tuple-element.125, bf16[1280,1408]{1,0:T(8,128)(2,1)S(1)} %copy-done.52), kind=kOutput, calls=%fused_computation.377 | convolution fusion | flops 7397703680 | bytes 20840448 | tf_op jit(solution)/shard_map/rf,df->rd/dot_general | solution.py:18
  359.9 15.7 %collective-permute-done.54 = bf16[128,2816]{1,0:T(8,128)(2,1)S(1)} collective-permute-done((bf16[128,2816]{1,0:T(8,128)(2,1)}, bf16[128,2816]{1,0:T(8,128)(2,1)S(1)}, u32[]{:S(2)}, u32[]{:S(2)}) %collective-permute-start.54) | collective-permute-done | bytes 720928 | tf_op jit(solution)/shard_map/ppermute | solution.py:461
  378.3 12.2 %collective-permute-done.56 = bf16[128,2816]{1,0:T(8,128)(2,1)S(1)} collective-permute-done((bf16[128,2816]{1,0:T(8,128)(2,1)}, bf16[128,2816]{1,0:T(8,128)(2,1)S(1)}, u32[]{:S(2)}, u32[]{:S(2)}) %collective-permute-start.56) | collective-permute-done | bytes 720928 | tf_op jit(solution)/shard_map/ppermute | solution.py:461
  391.1 14.2 %collective-permute-done.57 = bf16[128,2816]{1,0:T(8,128)(2,1)S(1)} collective-permute-done((bf16[128,2816]{1,0:T(8,128)(2,1)}, bf16[128,2816]{1,0:T(8,128)(2,1)S(1)}, u32[]{:S(2)}, u32[]{:S(2)}) %collective-permute-start.57) | collective-permute-done | bytes 720928 | tf_op jit(solution)/shard_map/ppermute | solution.py:461
  423.9 12.9 %collective-permute-done.61 = bf16[352,1024]{1,0:T(8,128)(2,1)S(1)} collective-permute-done((bf16[352,1024]{1,0:T(8,128)(2,1)S(1)}, bf16[352,1024]{1,0:T(8,128)(2,1)S(1)}, u32[]{:S(2)}, u32[]{:S(2)}) %collective-permute-start.61) | collective-permute-done | bytes 720928 | tf_op jit(solution)/shard_map/ppermute | solution.py:473
  453.3 10.9 %concatenate.102 = f32[1024,1029]{0,1:T(8,128)} concatenate(f32[1024,1024]{0,1:T(8,128)} %convolution_bitcast_fusion.1, f32[1024,4]{0,1:T(4,128)S(1)} %convolution_bitcast_fusion.2, f32[1024,1]{0,1:T(1,128)S(1)} %bitcast.400), dimensions={1} | concatenate | bytes 8429568 | tf_op jit(solution)/shard_map/concatenate | solution.py:530
  500.7 15.0 %shard_map.265 = (bf16[2,256,1536]{2,1,0:T(8,128)(2,1)S(1)}, f32[8,512]{1,0:T(8,128)S(1)}) custom-call(s32[2]{0:T(128)S(1)} %bitcast.340, f32[8,512]{1,0:T(8,128)S(1)} %pad_maximum_fusion.19.line_ref, bf16[2,256,1536]{2,1,0:T(8,128)(2,1)S(1)} %convolution_convert_fusion.1.qkv_ref, bf16[2,256,512]{2,1,0:T(8,128)(2,1)S(1)} %fusion.31.grad_ref), custom_call_target="tpu_custom_call" | custom-call | tf_op jit(solution)/shard_map/pallas_call | solution.py:148
  537.9 10.2 %copy.309 = f32[2,2,425984]{2,0,1:T(2,128)S(1)} copy(f32[2,2,425984]{2,1,0:T(2,128)} %reshape_reshape.12) | data formatting | bytes 13631488 | tf_op jit(solution)/shard_map/reshape;reshape | solution.py:180
  554.8 49.6 %psum.7 = f32[32,16]{0,1:T(8,128)} all-reduce(f32[32,16]{0,1:T(8,128)S(1)} %convolution_dynamic-update-slice_fusion), channel_id=1, replica_groups=mesh['dp'=4,'context'=2,'experts'=4] {'dp','context','experts'}, use_global_device_ids=true, to_apply=%region_18.19 | all-reduce | flops 512 | bytes 4096 | tf_op jit(solution)/shard_map/psum | solution.py:566
  613.9 24.5 %collective-permute-done.47 = bf16[1,294912]{1,0:T(2,128)(2,1)S(1)} collective-permute-done((bf16[1,294912]{1,0:T(2,128)(2,1)S(1)}, bf16[1,294912]{1,0:T(2,128)(2,1)S(1)}, u32[]{:S(2)}, u32[]{:S(2)}) %collective-permute-start.47) | collective-permute-done | bytes 589856 | tf_op jit(solution)/shard_map/ppermute | solution.py:23
  638.4 12.2 %fusion.39 = f32[294912]{0:T(1024)S(1)} fusion(pred[]{:T(512)S(6)} %eq.241, bf16[1,294912]{1,0:T(2,128)(2,1)S(1)} %collective-permute-done.47, f32[2,294912]{1,0:T(2,128)S(1)} %bitcast_add_fusion.1), kind=kLoop, calls=%fused_computation.97 | loop fusion | flops 884736 | bytes 4128769 | tf_op jit(solution)/shard_map/add | solution.py:172
  670.2 27.7 %collective-permute-done.42 = bf16[1,425984]{1,0:T(2,128)(2,1)S(1)} collective-permute-done((bf16[1,425984]{1,0:T(2,128)(2,1)S(1)}, bf16[1,425984]{1,0:T(2,128)(2,1)S(1)}, u32[]{:S(2)}, u32[]{:S(2)}) %collective-permute-start.42) | collective-permute-done | bytes 852000 | tf_op jit(solution)/shard_map/ppermute | solution.py:23
  697.9 17.9 %fusion.18 = f32[425984]{0:T(1024)S(1)} fusion(pred[]{:T(512)S(6)} %eq.241, bf16[1,425984]{1,0:T(2,128)(2,1)S(1)} %collective-permute-done.42, f32[2,425984]{1,0:T(2,128)S(1)} %bitcast_add_fusion), kind=kLoop, calls=%fused_computation.51 | loop fusion | flops 1277952 | bytes 5963777 | tf_op jit(solution)/shard_map/add | solution.py:172
  (420 shorter events, 342.4 us)
Async XLA Ops:
  7.2 106.0 %all-gather.6.cloned.1.call-start = ((), (), s32[]{:S(2)}) async-start(), calls=%async_computation.1 | async-start | bytes 3620864 | tf_op jit(solution)/shard_map/all_gather | solution.py:283
  16.6 132.4 %all-gather.4.cloned.1.call-start = ((), (), s32[]{:S(2)}) async-start(), calls=%async_computation | async-start | bytes 2162688 | tf_op jit(solution)/shard_map/all_gather | solution.py:290
  16.6 68.6 %collective-permute-start.14 = (bf16[352,1024]{1,0:T(8,128)(2,1)}, bf16[352,1024]{1,0:T(8,128)(2,1)}, u32[]{:S(2)}, u32[]{:S(2)}) collective-permute-start(bf16[352,1024]{1,0:T(8,128)(2,1)} %bitcast.420), channel_id=1, source_target_pairs={{0,0},{1,1},{2,2},{3,3},{4,4},{5,5},{6,6},{7,7},{8,16},{9,17},{10,... | collective-permute-start | bytes 2162696 | tf_op jit(solution)/shard_map/ppermute | solution.py:316
  23.5 63.5 %collective-permute-start.15 = (bf16[352,1024]{1,0:T(8,128)(2,1)}, bf16[352,1024]{1,0:T(8,128)(2,1)}, u32[]{:S(2)}, u32[]{:S(2)}) collective-permute-start(bf16[352,1024]{1,0:T(8,128)(2,1)} %bitcast.421), channel_id=1, source_target_pairs={{0,16},{1,17},{2,18},{3,19},{4,20},{5,21},{6,22},{7,23},{8,0},{9,1... | collective-permute-start | bytes 2162696 | tf_op jit(solution)/shard_map/ppermute | solution.py:316
  25.4 82.6 %collective-permute-start.16 = (bf16[352,1024]{1,0:T(8,128)(2,1)}, bf16[352,1024]{1,0:T(8,128)(2,1)}, u32[]{:S(2)}, u32[]{:S(2)}) collective-permute-start(bf16[352,1024]{1,0:T(8,128)(2,1)} %bitcast.422), channel_id=1, source_target_pairs={{0,4},{1,5},{2,6},{3,7},{4,0},{5,1},{6,2},{7,3},{8,20},{9,21},{10,... | collective-permute-start | bytes 2162696 | tf_op jit(solution)/shard_map/ppermute | solution.py:316
  27.2 83.0 %collective-permute-start.17 = (bf16[352,1024]{1,0:T(8,128)(2,1)}, bf16[352,1024]{1,0:T(8,128)(2,1)}, u32[]{:S(2)}, u32[]{:S(2)}) collective-permute-start(bf16[352,1024]{1,0:T(8,128)(2,1)} %bitcast.423), channel_id=1, source_target_pairs={{0,20},{1,21},{2,22},{3,23},{4,16},{5,17},{6,18},{7,19},{8,4},{9,5... | collective-permute-start | bytes 2162696 | tf_op jit(solution)/shard_map/ppermute | solution.py:316
  27.5 42.9 %collective-permute-start.23 = (bf16[2,128,1024]{2,1,0:T(8,128)(2,1)}, bf16[2,128,1024]{2,1,0:T(8,128)(2,1)}, u32[]{:S(2)}, u32[]{:S(2)}) collective-permute-start(bf16[2,128,1024]{2,1,0:T(8,128)(2,1)} %bitcast.374), channel_id=1, source_target_pairs={{0,4},{4,0},{1,5},{5,1},{2,6},{6,2},{3,7},{7,3},{8,12},{12,8},{9,1... | collective-permute-start | bytes 1572872 | tf_op jit(solution)/shard_map/ppermute | solution.py:23
  94.8 67.5 %collective-permute-start.12 = (bf16[128,2816]{1,0:T(8,128)(2,1)}, bf16[128,2816]{1,0:T(8,128)(2,1)}, u32[]{:S(2)}, u32[]{:S(2)}) collective-permute-start(bf16[128,2816]{1,0:T(8,128)(2,1)} %get-tuple-element.147), channel_id=1, source_target_pairs={{0,24},{8,16},{16,8},{24,0},{1,25},{9,17},{17,9},{25,1},{2,26},{10... | collective-permute-start | bytes 2162696 | tf_op jit(solution)/shard_map/ppermute | solution.py:23
  106.2 54.1 %collective-permute-start.9 = (bf16[128,2816]{1,0:T(8,128)(2,1)}, bf16[128,2816]{1,0:T(8,128)(2,1)}, u32[]{:S(2)}, u32[]{:S(2)}) collective-permute-start(bf16[128,2816]{1,0:T(8,128)(2,1)} %collective-permute-done.8), channel_id=1, source_target_pairs={{0,4},{4,0},{1,5},{5,1},{2,6},{6,2},{3,7},{7,3},{8,12},{12,8},{9,1... | collective-permute-start | bytes 2162696 | tf_op jit(solution)/shard_map/ppermute | solution.py:23
  108.1 79.7 %collective-permute-start.11 = (bf16[128,2816]{1,0:T(8,128)(2,1)}, bf16[128,2816]{1,0:T(8,128)(2,1)}, u32[]{:S(2)}, u32[]{:S(2)}) collective-permute-start(bf16[128,2816]{1,0:T(8,128)(2,1)} %collective-permute-done.10), channel_id=1, source_target_pairs={{0,4},{4,0},{1,5},{5,1},{2,6},{6,2},{3,7},{7,3},{8,12},{12,8},{9,1... | collective-permute-start | bytes 2162696 | tf_op jit(solution)/shard_map/ppermute | solution.py:23
  162.3 60.6 %collective-permute-start.27 = (bf16[2,80,1024]{2,1,0:T(8,128)(2,1)}, bf16[2,80,1024]{2,1,0:T(8,128)(2,1)}, u32[]{:S(2)}, u32[]{:S(2)}) collective-permute-start(bf16[2,80,1024]{2,1,0:T(8,128)(2,1)} %get-tuple-element.167), channel_id=1, source_target_pairs={{0,1},{1,0},{2,3},{3,2},{4,5},{5,4},{6,7},{7,6},{8,9},{9,8},{10,11... | collective-permute-start | bytes 983048 | tf_op jit(solution)/shard_map/ppermute | solution.py:23
  172.7 50.2 %collective-permute-start.28 = (bf16[2,80,1024]{2,1,0:T(8,128)(2,1)}, bf16[2,80,1024]{2,1,0:T(8,128)(2,1)}, u32[]{:S(2)}, u32[]{:S(2)}) collective-permute-start(bf16[2,80,1024]{2,1,0:T(8,128)(2,1)} %get-tuple-element.166), channel_id=1, source_target_pairs={{0,2},{1,3},{2,0},{3,1},{4,6},{5,7},{6,4},{7,5},{8,10},{9,11},{10,... | collective-permute-start | bytes 983048 | tf_op jit(solution)/shard_map/ppermute | solution.py:23
  187.7 35.2 %collective-permute-start.29 = (bf16[2,80,1024]{2,1,0:T(8,128)(2,1)}, bf16[2,80,1024]{2,1,0:T(8,128)(2,1)}, u32[]{:S(2)}, u32[]{:S(2)}) collective-permute-start(bf16[2,80,1024]{2,1,0:T(8,128)(2,1)} %get-tuple-element.165), channel_id=1, source_target_pairs={{0,3},{1,2},{2,1},{3,0},{4,7},{5,6},{6,5},{7,4},{8,11},{9,10},{10,... | collective-permute-start | bytes 983048 | tf_op jit(solution)/shard_map/ppermute | solution.py:23
  345.7 44.8 %collective-permute-start.56 = (bf16[128,2816]{1,0:T(8,128)(2,1)}, bf16[128,2816]{1,0:T(8,128)(2,1)S(1)}, u32[]{:S(2)}, u32[]{:S(2)}) collective-permute-start(bf16[128,2816]{1,0:T(8,128)(2,1)} %get-tuple-element.130), channel_id=1, source_target_pairs={{0,16},{1,17},{2,18},{3,19},{4,20},{5,21},{6,22},{7,23},{8,24},{9,... | collective-permute-start | bytes 2162696 | tf_op jit(solution)/shard_map/ppermute | solution.py:461
  346.2 59.0 %collective-permute-start.57 = (bf16[128,2816]{1,0:T(8,128)(2,1)}, bf16[128,2816]{1,0:T(8,128)(2,1)S(1)}, u32[]{:S(2)}, u32[]{:S(2)}) collective-permute-start(bf16[128,2816]{1,0:T(8,128)(2,1)} %get-tuple-element.129), channel_id=1, source_target_pairs={{0,20},{1,21},{2,22},{3,23},{4,16},{5,17},{6,18},{7,19},{8,28},{9,... | collective-permute-start | bytes 2162696 | tf_op jit(solution)/shard_map/ppermute | solution.py:461
  359.2 60.1 %collective-permute-start.58 = (bf16[352,1024]{1,0:T(8,128)(2,1)S(1)}, bf16[352,1024]{1,0:T(8,128)(2,1)S(1)}, u32[]{:S(2)}, u32[]{:S(2)}) collective-permute-start(bf16[352,1024]{1,0:T(8,128)(2,1)S(1)} %get-tuple-element.135), channel_id=1, source_target_pairs={{0,0},{1,1},{2,2},{3,3},{4,4},{5,5},{6,6},{7,7},{16,8},{17,9},{18,... | collective-permute-start | bytes 2162696 | tf_op jit(solution)/shard_map/ppermute | solution.py:473
  375.6 45.7 %collective-permute-start.59 = (bf16[352,1024]{1,0:T(8,128)(2,1)S(1)}, bf16[352,1024]{1,0:T(8,128)(2,1)S(1)}, u32[]{:S(2)}, u32[]{:S(2)}) collective-permute-start(bf16[352,1024]{1,0:T(8,128)(2,1)S(1)} %get-tuple-element.138), channel_id=1, source_target_pairs={{16,0},{17,1},{18,2},{19,3},{20,4},{21,5},{22,6},{23,7},{0,8},{1,9... | collective-permute-start | bytes 2162696 | tf_op jit(solution)/shard_map/ppermute | solution.py:473
  377.5 46.4 %collective-permute-start.60 = (bf16[352,1024]{1,0:T(8,128)(2,1)S(1)}, bf16[352,1024]{1,0:T(8,128)(2,1)S(1)}, u32[]{:S(2)}, u32[]{:S(2)}) collective-permute-start(bf16[352,1024]{1,0:T(8,128)(2,1)S(1)} %get-tuple-element.137), channel_id=1, source_target_pairs={{4,0},{5,1},{6,2},{7,3},{0,4},{1,5},{2,6},{3,7},{20,8},{21,9},{22,... | collective-permute-start | bytes 2162696 | tf_op jit(solution)/shard_map/ppermute | solution.py:473
  390.5 46.2 %collective-permute-start.61 = (bf16[352,1024]{1,0:T(8,128)(2,1)S(1)}, bf16[352,1024]{1,0:T(8,128)(2,1)S(1)}, u32[]{:S(2)}, u32[]{:S(2)}) collective-permute-start(bf16[352,1024]{1,0:T(8,128)(2,1)S(1)} %get-tuple-element.136), channel_id=1, source_target_pairs={{20,0},{21,1},{22,2},{23,3},{16,4},{17,5},{18,6},{19,7},{4,8},{5,9... | collective-permute-start | bytes 2162696 | tf_op jit(solution)/shard_map/ppermute | solution.py:473
  496.9 107.5 %collective-permute-start.46 = (bf16[2,294912]{1,0:T(2,128)(2,1)}, bf16[2,294912]{1,0:T(2,128)(2,1)}, u32[]{:S(2)}, u32[]{:S(2)}) collective-permute-start(bf16[2,294912]{1,0:T(2,128)(2,1)} %bitcast.337), channel_id=1, source_target_pairs={{0,8},{8,0},{16,24},{24,16},{1,9},{9,1},{17,25},{25,17},{2,10},{10... | collective-permute-start | bytes 3538952 | tf_op jit(solution)/shard_map/ppermute | solution.py:23
  496.9 166.2 %collective-permute-start.38 = (bf16[2,128,1024]{2,1,0:T(8,128)(2,1)}, bf16[2,128,1024]{2,1,0:T(8,128)(2,1)}, u32[]{:S(2)}, u32[]{:S(2)}) collective-permute-start(bf16[2,128,1024]{2,1,0:T(8,128)(2,1)} %get-tuple-element.96), channel_id=1, source_target_pairs={{0,4},{4,0},{1,5},{5,1},{2,6},{6,2},{3,7},{7,3},{8,12},{12,8},{9,1... | collective-permute-start | bytes 1572872 | tf_op jit(solution)/shard_map/ppermute | solution.py:23
  552.1 101.1 %collective-permute-start.41 = (bf16[2,425984]{1,0:T(2,128)(2,1)}, bf16[2,425984]{1,0:T(2,128)(2,1)}, u32[]{:S(2)}, u32[]{:S(2)}) collective-permute-start(bf16[2,425984]{1,0:T(2,128)(2,1)} %fusion.20), channel_id=1, source_target_pairs={{0,8},{8,0},{16,24},{24,16},{1,9},{9,1},{17,25},{25,17},{2,10},{10... | collective-permute-start | bytes 5111816 | tf_op jit(solution)/shard_map/ppermute | solution.py:23
  553.5 60.0 %collective-permute-start.40 = (bf16[2,128,1024]{2,1,0:T(8,128)(2,1)S(1)}, bf16[2,128,1024]{2,1,0:T(8,128)(2,1)S(1)}, u32[]{:S(2)}, u32[]{:S(2)}) collective-permute-start(bf16[2,128,1024]{2,1,0:T(8,128)(2,1)S(1)} %dynamic-slice_convert_fusion.4), channel_id=1, source_target_pairs={{0,4},{4,0},{1,5},{5,1},{2,6},{6,2},{3,7},{7,3},{8,12},{12,8},{9,1... | collective-permute-start | bytes 1572872 | tf_op jit(solution)/shard_map/ppermute | solution.py:23
  660.8 37.1 %collective-permute-start.42 = (bf16[1,425984]{1,0:T(2,128)(2,1)S(1)}, bf16[1,425984]{1,0:T(2,128)(2,1)S(1)}, u32[]{:S(2)}, u32[]{:S(2)}) collective-permute-start(bf16[1,425984]{1,0:T(2,128)(2,1)S(1)} %fusion.19), channel_id=1, source_target_pairs={{0,16},{8,24},{16,0},{24,8},{1,17},{9,25},{17,1},{25,9},{2,18},{10... | collective-permute-start | bytes 2555912 | tf_op jit(solution)/shard_map/ppermute | solution.py:23
  (95 other events, 1222.3 us)
Sparse Core Ops, SparseCore 0:
  16.7 54.7 all-gather.5
  74.4 60.4 all-gather.3
where the time goes:
time: 758 us; the launch traced here: 749 us
  waiting for transfers between devices  255 us (34%)
  local copies, waits for them, and re-layouts  106 us (14%)
  starting transfers between devices  106 us (14%)
  other arithmetic  98.6 us (13%)
  matrix products  94.6 us (12%)
  blocking collectives  49.6 us (7%)
  Pallas kernels  23.3 us (3%)
  between operations  16.1 us (2%)
    ppermute x47, waiting for transfers between devices, swap(): return lax.ppermute(value, axis, [(i, i ^ offset) for i in range(size)])  193 us
    dot_general x32, matrix products, dot_f32(): return jnp.einsum(spec, left, right, preferred_element_type=F32)  94.4 us
    ppermute x47, starting transfers between devices, swap(): return lax.ppermute(value, axis, [(i, i ^ offset) for i in range(size)])  83.1 us
    psum x1, blocking collectives, body(): grad_table = lax.psum(table_full, ALL)  49.6 us
    ppermute x7, waiting for transfers between devices, body(): block = lax.ppermute(block, ALL, pairs)  47.1 us
    add x6, other arithmetic, halve(): return kept + swap(sent, axis, bit).astype(F32)  40.9 us
    unnamed x125, local copies, waits for them, and re-layouts  32.7 us
    another operation x3, local copies, waits for them, and re-layouts, scatter_sum(): shaped = value.reshape((count // 2, 2, -1))  24.4 us
  transfers between devices with their start and end apart: 64, of which 25 were waited for; matrix products, arithmetic and copies ran while one was open for 25% of the time, Pallas kernels for 3%

commit v1 on v0

--- a/solution.py
+++ b/solution.py
@@ -189,6 +189,235 @@
         count //= 2
         bit *= 2
     return value.reshape((ctx_count,) + rest)
+
+
+MESH = pl.DeviceIdType.MESH
+
+
+def flip(index, bit):
+    return index + bit - 2 * bit * ((index // bit) % 2)
+
+
+def greet(targets):
+    barrier = pltpu.get_barrier_semaphore()
+    for target in targets:
+        pl.semaphore_signal(barrier, inc=1, device_id=target, device_id_type=MESH)
+    pl.semaphore_wait(barrier, len(targets))
+
+
+def remote(source, place, sends, receives, target):
+    return pltpu.make_async_remote_copy(
+        src_ref=source,
+        dst_ref=place,
+        send_sem=sends,
+        recv_sem=receives,
+        device_id=target,
+        device_id_type=MESH,
+    )
+
+
+def reduce_kernel(
+    own_width,
+    qkv_ref,
+    out_ref,
+    small_ref,
+    diag_ref,
+    query_out,
+    key_out,
+    value_out,
+    out_out,
+    small_out,
+    diag_out,
+    *scratch,
+):
+    dp, ctx, exp = (lax.axis_index(name) for name in ALL)
+    high, low = dp // 2, dp % 2
+    z_high, z_low = exp // 2, exp % 2
+    peers = [
+        (flip(dp, 1), ctx, exp),
+        (flip(dp, 2), ctx, exp),
+        (dp, ctx, flip(exp, 1)),
+        (dp, ctx, flip(exp, 2)),
+        (dp, 1 - ctx, exp),
+    ]
+    chunks = []
+    for c in range(3):
+        chunks.append((qkv_ref, c * own_width, own_width))
+    width = out_ref.shape[-1]
+    for c in range(width // own_width):
+        chunks.append((out_ref, c * own_width, own_width))
+    chunks.append((small_ref, 0, small_ref.shape[-1]))
+    count = len(chunks)
+    per = 9
+    bufs = [scratch[i * per : (i + 1) * per] for i in range(count)]
+    diag_buf, sends, receives, diag_sends, diag_receives = scratch[count * per :]
+    greet(peers)
+
+    flying = []
+
+    def launch(i, stage, source, place):
+        copy = remote(source, place, sends.at[i, stage], receives.at[i, stage], peers[stage])
+        copy.start()
+        flying.append(copy)
+        return copy
+
+    copies = {}
+    for i, (ref, start, size) in enumerate(chunks):
+        copies[i, 0] = launch(
+            i, 0, ref.at[:, 1 - low, :, start : start + size], bufs[i][0]
+        )
+    diag_buf[0] = diag_ref[...]
+    diag_copies = []
+
+    def diag_step(stage):
+        if stage:
+            diag_copies[stage - 1].wait_recv()
+        if stage and stage < 5:
+            diag_buf[2 * stage] = diag_buf[2 * stage - 2] + diag_buf[2 * stage - 1]
+        if stage < 5:
+            copy = remote(
+                diag_buf.at[2 * stage],
+                diag_buf.at[2 * stage + 1],
+                diag_sends.at[stage],
+                diag_receives.at[stage],
+                peers[stage],
+            )
+            copy.start()
+            diag_copies.append(copy)
+            flying.append(copy)
+
+    def advance(i, stage):
+        ref, start, size = chunks[i]
+        recv_a, send_b, recv_b, send_c, recv_c, send_d, recv_d, send_e, recv_e = bufs[i]
+        copies[i, stage].wait_recv()
+        if stage == 0:
+            send_b[...] = (
+                ref[1 - high, low, :, start : start + size].astype(F32)
+                + recv_a[1 - high].astype(F32)
+            ).astype(BF16)
+            copies[i, 1] = launch(i, 1, send_b, recv_b)
+        elif stage == 1:
+            total = (
+                ref[high, low, :, start : start + size].astype(F32)
+                + recv_a[high].astype(F32)
+                + recv_b[...].astype(F32)
+            ).astype(BF16)
+            send_c[...] = total.reshape(send_c.shape)
+            copies[i, 2] = launch(i, 2, send_c.at[:, :, 1 - z_low], recv_c)
+        elif stage == 2:
+            send_d[...] = (
+                send_c[:, :, z_low].astype(F32) + recv_c[...].astype(F32)
+            ).astype(BF16)
+            copies[i, 3] = launch(i, 3, send_d.at[:, 1 - z_high], recv_d)
+        elif stage == 3:
+            send_e[...] = (send_d[:, z_high].astype(F32) + recv_d[...].astype(F32)).astype(BF16)
+            copies[i, 4] = launch(i, 4, send_e.at[1 - ctx], recv_e)
+        else:
+            mine, other = send_e[ctx].astype(F32), recv_e[...].astype(F32)
+            if i < 3:
+                place = (query_out, key_out, value_out)[i]
+                place[:, pl.ds(pl.multiple_of(ctx * size, 128), size)] = mine
+                place[:, pl.ds(pl.multiple_of((1 - ctx) * size, 128), size)] = other
+            elif ref is out_ref:
+                out_out[:, start : start + size] = mine + other
+            else:
+                small_out[...] = mine + other
+
+    for step in range(count + 4):
+        if step < 6:
+            diag_step(step)
+        for stage in range(4, -1, -1):
+            if 0 <= step - stage < count:
+                advance(step - stage, stage)
+    diag_out[ctx] = diag_buf[8]
+    diag_out[1 - ctx] = diag_buf[9]
+    for copy in flying:
+        copy.wait_send()
+
+
+def reduce_dense(qkv_total, out_total, small, diagonals, own_width):
+    rows, width = out_total.shape
+    dp_count, ctx_count, expert_count = (lax.axis_size(name) for name in ALL)
+    per_row = rows // (dp_count * ctx_count * expert_count)
+    shaped = lambda v: v.reshape((2, 2, rows // 4, v.shape[-1]))
+    sizes = [own_width] * (3 + width // own_width) + [small.shape[-1]]
+    scratch = []
+    quarter = rows // 4
+    for size in sizes:
+        scratch += [
+            pltpu.VMEM((2, quarter, size), BF16),
+            pltpu.VMEM((quarter, size), BF16),
+            pltpu.VMEM((quarter, size), BF16),
+            pltpu.VMEM((2, 2, 2, per_row, size), BF16),
+            pltpu.VMEM((2, 2, per_row, size), BF16),
+            pltpu.VMEM((2, 2, per_row, size), BF16),
+            pltpu.VMEM((2, per_row, size), BF16),
+            pltpu.VMEM((2, per_row, size), BF16),
+            pltpu.VMEM((per_row, size), BF16),
+        ]
+    scratch += [
+        pltpu.VMEM((10,) + diagonals.shape, F32),
+        pltpu.SemaphoreType.DMA((len(sizes), 5)),
+        pltpu.SemaphoreType.DMA((len(sizes), 5)),
+        pltpu.SemaphoreType.DMA((5,)),
+        pltpu.SemaphoreType.DMA((5,)),
+    ]
+    whole = pl.BlockSpec(memory_space=pltpu.VMEM)
+    return pl.pallas_call(
+        functools.partial(reduce_kernel, own_width),
+        out_shape=tuple(jax.ShapeDtypeStruct((per_row, width), F32) for _ in range(4))
+        + (
+            jax.ShapeDtypeStruct((per_row, small.shape[-1]), F32),
+            jax.ShapeDtypeStruct((2,) + diagonals.shape, F32),
+        ),
+        in_specs=[whole] * 4,
+        out_specs=(whole,) * 6,
+        scratch_shapes=scratch,
+        compiler_params=pltpu.CompilerParams(
+            collective_id=0, has_side_effects=True, vmem_limit_bytes=48 * 2**20
+        ),
+    )(shaped(qkv_total), shaped(out_total), shaped(small), diagonals)
+
+
+def plain_sums(qkv_total, out_total, router_total, first_total, second_total, own_width):
+    width, experts = router_total.shape
+    dp_count, ctx_count, expert_count = (lax.axis_size(name) for name in ALL)
+    dp_index, ctx_index, expert_index = (lax.axis_index(name) for name in ALL)
+    owners = (dp_count, ctx_count, expert_count, -1)
+    out_pack = jnp.concatenate([out_total, router_total, second_total[:, None]], axis=1)
+    out_pack = jnp.pad(out_pack, ((0, 0), (0, width + 128 - out_pack.shape[1])))
+    out_pack = scatter_sum(
+        out_pack.reshape(owners + (out_pack.shape[1],)), dp_index, expert_index
+    )
+    qkv_pack = jnp.pad(
+        jnp.concatenate([qkv_total, first_total[:, None]], axis=1), ((0, 0), (0, 127))
+    )
+    qkv_pack = scatter_sum(
+        qkv_pack.reshape(owners + (qkv_pack.shape[1],)), dp_index, expert_index
+    )
+
+    def across(value):
+        parts = reorder([value[c] for c in range(ctx_count)], ctx_index)
+        return [parts[0]] + [
+            swap(parts[k].astype(BF16), "context", k).astype(F32) for k in range(1, ctx_count)
+        ]
+
+    out_sum = sum(across(out_pack))
+    qkv_parts = across(qkv_pack)
+    grad_first = sum(part[:, 3 * own_width] for part in qkv_parts)
+    qkv_parts = reorder(qkv_parts, ctx_index)
+    grads = tuple(
+        jnp.concatenate(
+            [part[:, i * own_width : (i + 1) * own_width] for part in qkv_parts], axis=1
+        )
+        for i in range(3)
+    )
+    return grads + (
+        out_sum[:, :width],
+        out_sum[:, width : width + experts],
+        grad_first,
+        out_sum[:, width + experts],
+    )
 
 
 def norm_pull(features, inverse, gain, grad):
@@ -260,6 +489,12 @@
     weight_rows = w_query.shape[0]
     plane = dp_count * ctx_count
     plane_index = dp_index * ctx_count + ctx_index
+    tuned = (
+        (dp_count, ctx_count, expert_count) == (4, 2, 4)
+        and weight_rows % 16 == 0
+        and own_width % 128 == 0
+        and width % own_width == 0
+    )
     act = activations[:, 0]
     cot = cotangent[:, 0]
     deal = dealing[:, 0]
@@ -526,44 +761,30 @@
     grad_input = (to_positions(hidden_low) + rows_back).astype(BF16)[:, None]
     output = to_positions(final).astype(BF16)[:, None]
 
-    owners = (dp_count, ctx_count, expert_count, weight_rows)
-    out_pack = jnp.concatenate(
-        [out_total, router_total, second_total[:, None]], axis=1
-    )
-    out_pack = jnp.pad(out_pack, ((0, 0), (0, width + 128 - out_pack.shape[1])))
-    out_pack = scatter_sum(out_pack.reshape(owners + (-1,)), dp_index, expert_index)
-    qkv_pack = jnp.pad(
-        jnp.concatenate([qkv_total, first_total[:, None]], axis=1), ((0, 0), (0, 127))
-    )
-    qkv_pack = scatter_sum(qkv_pack.reshape(owners + (-1,)), dp_index, expert_index)
-
-    def across(value):
-        parts = reorder([value[c] for c in range(ctx_count)], ctx_index)
-        return [parts[0]] + [
-            swap(parts[k].astype(BF16), "context", k).astype(F32) for k in range(1, ctx_count)
-        ]
-
-    out_sum = sum(across(out_pack))
-    qkv_parts = across(qkv_pack)
-    grad_first = sum(part[:, 3 * own_width] for part in qkv_parts)
-    qkv_parts = reorder(qkv_parts, ctx_index)
-    grad_query, grad_key, grad_value = (
-        jnp.concatenate(
-            [part[:, i * own_width : (i + 1) * own_width] for part in qkv_parts], axis=1
+    if tuned:
+        small = jnp.concatenate(
+            [router_total, second_total[:, None], first_total[:, None]], axis=1
         )
-        for i in range(3)
-    )
-    grad_out = out_sum[:, :width]
-    grad_router = out_sum[:, width : width + experts]
-    grad_second = out_sum[:, width + experts]
-    offsets = jnp.concatenate([diagonals[:, :1], diagonals[:, : seq : -1]], axis=1)
-    table_part = jnp.einsum(
+        small = jnp.pad(small, ((0, 0), (0, 128 - small.shape[1]))).astype(BF16)
+        grad_query, grad_key, grad_value, grad_out, small_sum, diag_all = reduce_dense(
+            qkv_total.astype(BF16), out_total.astype(BF16), small, diagonals, own_width
+        )
+        grad_router = small_sum[:, :experts]
+        grad_second = small_sum[:, experts]
+        grad_first = small_sum[:, experts + 1]
+        diag_all = diag_all.reshape((head_count, -1))
+    else:
+        sums = plain_sums(
+            qkv_total, out_total, router_total, first_total, second_total, own_width
+        )
+        grad_query, grad_key, grad_value, grad_out, grad_router, grad_first, grad_second = sums
+        diag_all = lax.all_gather(
+            lax.psum(diagonals, ("dp", "experts")), "context", axis=0, tiled=True
+        )
+    offsets = jnp.concatenate([diag_all[:, :1], diag_all[:, : seq : -1]], axis=1)
+    grad_table = jnp.einsum(
         "hs,sb->bh", offsets, bucket_hot.astype(F32), precision=lax.Precision.HIGHEST
     )
-    table_full = lax.dynamic_update_slice(
-        jnp.zeros(bias_table.shape, F32), table_part, (0, ctx_index * heads)
-    )
-    grad_table = lax.psum(table_full, ALL)
     return (
         output,
         grad_input,

time: 758 us -> 568 us (0.75)
  other arithmetic: 98.6 us -> 25.7 us
  waiting for transfers between devices: 255 us -> 192 us
  Pallas kernels: 23.3 us -> 83.5 us
  blocking collectives: 49.6 us -> 0 us
  local copies, waits for them, and re-layouts: 106 us -> 59.6 us
  starting transfers between devices: 106 us -> 93.2 us
    ppermute x47 -> x37, waiting for transfers between devices: 193 us -> 130 us  [swap(): return lax.ppermute(value, axis, [(i, i ^ offset) for i in range(size)])]
    pallas_call x0 -> x1, Pallas kernels: none -> 60.4 us  [reduce_dense(): pl.pallas_call(functools.partial(reduce_kernel, own_width), out_shape=tup...]
    psum x1 -> x0, blocking collectives: 49.6 us -> none  [body(): grad_table = lax.psum(table_full, ALL)]
    add x8 -> x0, other arithmetic: 41.6 us -> none  [the longest x6 40.9 us: halve(): return kept + swap(sent, axis, bit).astype(F32)]
    another operation x5 -> x0, local copies, waits for them, and re-layouts: 24.9 us -> none  [the longest x3 24.4 us: scatter_sum(): shaped = value.reshape((count // 2, 2, -1))]
    convert_element_type x11 -> x0, other arithmetic: 16 us -> none  [the longest x8 15 us: halve(): sent = jnp.where(flag, value[0], value[1]).astype(BF16)]
    ppermute x47 -> x37, starting transfers between devices: 83.1 us -> 70.5 us  [swap(): return lax.ppermute(value, axis, [(i, i ^ offset) for i in range(size)])]
    concatenate x1 -> x0, local copies, waits for them, and re-layouts: 10.9 us -> none  [body(): jnp.concatenate([out_total, router_total, second_total[:, None]], axis=1)]
  transfers between devices with their start and end apart: 64 -> 54, of which waited for: 25 -> 20; matrix products, arithmetic and copies ran while one was open for 25% -> 20% of each run, Pallas kernels for 3% -> 15%
where the time goes in v1:
time: 568 us; the launch traced here: 559 us
  waiting for transfers between devices  192 us (34%)
  starting transfers between devices  93.2 us (16%)
  matrix products  89.1 us (16%)
  Pallas kernels  83.5 us (15%)
  local copies, waits for them, and re-layouts  59.6 us (10%)
  other arithmetic  25.7 us (5%)
  between operations  15.8 us (3%)
    ppermute x37, waiting for transfers between devices, swap(): return lax.ppermute(value, axis, [(i, i ^ offset) for i in range(size)])  130 us
    dot_general x32, matrix products, dot_f32(): return jnp.einsum(spec, left, right, preferred_element_type=F32)  88.2 us
    ppermute x37, starting transfers between devices, swap(): return lax.ppermute(value, axis, [(i, i ^ offset) for i in range(size)])  70.5 us
    pallas_call x1, Pallas kernels, reduce_dense(): pl.pallas_call(functools.partial(reduce_kernel, own_width), out_shape=tup...  60.4 us
    ppermute x7, waiting for transfers between devices, body(): block = lax.ppermute(block, ALL, pairs)  47.3 us
    unnamed x114, local copies, waits for them, and re-layouts  29.4 us
    pallas_call x1, Pallas kernels, attend_back(): pl.pallas_call(functools.partial(attend_back_kernel, heads, head_size), g...  15 us
    ppermute x4, waiting for transfers between devices, body(): arrived = lax.ppermute(piece, ALL, [(b, a) for a, b in pairs])  15 us
  transfers between devices with their start and end apart: 54, of which 20 were waited for; matrix products, arithmetic and copies ran while one was open for 20% of the time, Pallas kernels for 15%

profile of v1, /device:TPU:0, one launch (start us, length us, event | category | flops | bytes accessed | tf_op | source)
XLA Modules:
  0.0 559.1 jit_solution(15471050955290768888)
XLA Ops:
  16.6 6.9 %collective-permute-start.14 = (bf16[352,1024]{1,0:T(8,128)(2,1)}, bf16[352,1024]{1,0:T(8,128)(2,1)}, u32[]{:S(2)}, u32[]{:S(2)}) collective-permute-start(bf16[352,1024]{1,0:T(8,128)(2,1)} %bitcast.276), channel_id=1, source_target_pairs={{0,0},{1,1},{2,2},{3,3},{4,4},{5,5},{6,6},{7,7},{8,16},{9,17},{10,... | collective-permute-start | bytes 2162696 | tf_op jit(solution)/shard_map/ppermute | solution.py:551
  36.7 33.8 %collective-permute-done.23 = bf16[2,128,1024]{2,1,0:T(8,128)(2,1)} collective-permute-done((bf16[2,128,1024]{2,1,0:T(8,128)(2,1)}, bf16[2,128,1024]{2,1,0:T(8,128)(2,1)}, u32[]{:S(2)}, u32[]{:S(2)}) %collective-permute-start.23) | collective-permute-done | bytes 524320 | tf_op jit(solution)/shard_map/ppermute | solution.py:23
  76.0 9.1 %collective-permute-done = bf16[2,128,1024]{2,1,0:T(8,128)(2,1)S(1)} collective-permute-done((bf16[2,128,1024]{2,1,0:T(8,128)(2,1)S(1)}, bf16[2,128,1024]{2,1,0:T(8,128)(2,1)S(1)}, u32[]{:S(2)}, u32[]{:S(2)}) %collective-permute-start) | collective-permute-done | bytes 524320 | tf_op jit(solution)/shard_map/ppermute | solution.py:23
  96.2 9.9 %collective-permute-done.10 = bf16[128,2816]{1,0:T(8,128)(2,1)S(1)} collective-permute-done((bf16[128,2816]{1,0:T(8,128)(2,1)S(1)}, bf16[128,2816]{1,0:T(8,128)(2,1)S(1)}, u32[]{:S(2)}, u32[]{:S(2)}) %collective-permute-start.10) | collective-permute-done | bytes 720928 | tf_op jit(solution)/shard_map/ppermute | solution.py:23
  119.0 8.0 %shard_map.264 = bf16[2,256,512]{2,1,0:T(8,128)(2,1)S(1)} custom-call(s32[2]{0:T(128)S(1)} %bitcast.205, f32[8,512]{1,0:T(8,128)S(1)} %pad_maximum_fusion.16.line_ref, bf16[2,256,1536]{2,1,0:T(8,128)(2,1)S(1)} %convolution_convert_fusion.1.qkv_ref), custom_call_target="tpu_custom_call" | custom-call | tf_op jit(solution)/shard_map/pallas_call | solution.py:79
  132.4 16.1 %collective-permute-done.2 = bf16[2,128,512]{2,1,0:T(8,128)(2,1)S(1)} collective-permute-done((bf16[2,128,512]{2,1,0:T(8,128)(2,1)S(1)}, bf16[2,128,512]{2,1,0:T(8,128)(2,1)S(1)}, u32[]{:S(2)}, u32[]{:S(2)}) %collective-permute-start.2) | collective-permute-done | bytes 262176 | tf_op jit(solution)/shard_map/ppermute | solution.py:23
  161.6 9.4 %collective-permute-done.3 = bf16[2,80,1024]{2,1,0:T(8,128)(2,1)S(1)} collective-permute-done((bf16[2,80,1024]{2,1,0:T(8,128)(2,1)S(1)}, bf16[2,80,1024]{2,1,0:T(8,128)(2,1)S(1)}, u32[]{:S(2)}, u32[]{:S(2)}) %collective-permute-start.3) | collective-permute-done | bytes 327712 | tf_op jit(solution)/shard_map/ppermute | solution.py:23
  172.2 9.5 %collective-permute-done.4 = bf16[2,80,1024]{2,1,0:T(8,128)(2,1)S(1)} collective-permute-done((bf16[2,80,1024]{2,1,0:T(8,128)(2,1)S(1)}, bf16[2,80,1024]{2,1,0:T(8,128)(2,1)S(1)}, u32[]{:S(2)}, u32[]{:S(2)}) %collective-permute-start.4) | collective-permute-done | bytes 327712 | tf_op jit(solution)/shard_map/ppermute | solution.py:23
  195.2 10.3 %fusion.114 = f32[1280,2816]{1,0:T(8,128)S(1)} fusion(bf16[1024,2816]{1,0:T(8,128)(2,1)} %constant_dynamic-update-slice_fusion, bf16[640,256]{1,0:T(8,128)(2,1)S(1)} %get-tuple-element.182, bf16[640,256]{1,0:T(8,128)(2,1)S(1)} %get-tuple-element.183, bf16[640,256]{1,0:T(8,128)(2,1)S(1)} %get-tuple-element.184, ...), kind=kOutput, calls=%fused_computation.300 | convolution fusion | flops 7395082240 | bytes 22806528 | tf_op jit(solution)/shard_map/rd,df->rf/dot_general | solution.py:18
  210.6 7.5 %fusion.134 = f32[1280,1024]{1,0:T(8,128)S(1)} fusion(bf16[1280,1408]{1,0:T(8,128)(2,1)S(1)} %multiply_convert_fusion.2, bf16[1408,1024]{1,0:T(8,128)(2,1)} %constant_dynamic-update-slice_fusion.8), kind=kOutput, calls=%fused_computation.319 | convolution fusion | flops 3690987520 | bytes 11730944 | tf_op jit(solution)/shard_map/rf,fd->rd/dot_general | solution.py:18
  228.3 17.2 %collective-permute-start.35 = (f32[2,80]{1,0:T(2,128)S(1)}, f32[2,80]{1,0:T(2,128)S(1)}, u32[]{:S(2)}, u32[]{:S(2)}) collective-permute-start(f32[2,80]{1,0:T(2,128)S(1)} %squeeze.114), channel_id=1, source_target_pairs={{0,1},{1,0},{2,3},{3,2},{4,5},{5,4},{6,7},{7,6},{8,9},{9,8},{10,11... | collective-permute-start | bytes 1928 | tf_op jit(solution)/shard_map/ppermute | solution.py:23
  257.6 8.5 %collective-permute-done.24 = f32[2,80]{1,0:T(2,128)S(1)} collective-permute-done((f32[2,80]{1,0:T(2,128)S(1)}, f32[2,80]{1,0:T(2,128)S(1)}, u32[]{:S(2)}, u32[]{:S(2)}) %collective-permute-start.24) | collective-permute-done | bytes 672 | tf_op jit(solution)/shard_map/ppermute | solution.py:23
  269.4 7.6 %collective-permute-done.21 = bf16[2,80,1024]{2,1,0:T(8,128)(2,1)} collective-permute-done((bf16[2,80,1024]{2,1,0:T(8,128)(2,1)}, bf16[2,80,1024]{2,1,0:T(8,128)(2,1)}, u32[]{:S(2)}, u32[]{:S(2)}) %collective-permute-start.21) | collective-permute-done | bytes 327712 | tf_op jit(solution)/shard_map/ppermute | solution.py:23
  281.8 9.7 %collective-permute-done.22 = bf16[2,128,1024]{2,1,0:T(8,128)(2,1)S(1)} collective-permute-done((bf16[2,128,1024]{2,1,0:T(8,128)(2,1)S(1)}, bf16[2,128,1024]{2,1,0:T(8,128)(2,1)S(1)}, u32[]{:S(2)}, u32[]{:S(2)}) %collective-permute-start.22) | collective-permute-done | bytes 524320 | tf_op jit(solution)/shard_map/ppermute | solution.py:23
  292.7 15.5 %multiply_convert_fusion.1 = (bf16[1280,1408]{1,0:T(8,128)(2,1)}, bf16[1280,1408]{1,0:T(8,128)(2,1)}) fusion(f32[1280,2816]{1,0:T(8,128)} %copy-done.6, bf16[1408,1024]{1,0:T(8,128)(2,1)} %constant_dynamic-update-slice_fusion.8, bf16[640,1024]{1,0:T(8,128)(2,1)S(1)} %collective-permute-done.30, bf16[640,1024]{1,0:T(8,128)(2,1)S(1)} %fusion.2), kind=kOutput, calls=%fused_computation.3 | convolution fusion | flops 3735879680 | bytes 27131904 | tf_op jit(solution)/shard_map/rd,fd->rf/dot_general | solution.py:18
  308.3 11.0 %convolution_convert_fusion = bf16[1024,2816]{1,0:T(8,128)(2,1)S(1)} fusion(bf16[1280,1408]{1,0:T(8,128)(2,1)} %get-tuple-element.150, bf16[1280,1408]{1,0:T(8,128)(2,1)} %get-tuple-element.149, bf16[640,256]{1,0:T(8,128)(2,1)S(1)} %copy-done.37, bf16[640,256]{1,0:T(8,128)(2,1)S(1)} %copy-done.39, bf16[640,256]{1,0:T(8,128)(2,1)S(1)} %copy-done.41, ...), kind=kOutput, calls=%fused_computation.8 | convolution fusion | flops 7412383744 | bytes 15597568 | tf_op jit(solution)/shard_map/rd,rf->df/dot_general | solution.py:18
  322.8 13.1 %fusion.133 = (bf16[1280,1024]{1,0:T(8,128)(2,1)}, f32[1280,1024]{1,0:T(8,128)}) fusion(bf16[1024,2816]{1,0:T(8,128)(2,1)} %constant_dynamic-update-slice_fusion, bf16[1280,1408]{1,0:T(8,128)(2,1)} %get-tuple-element.150, bf16[1280,1408]{1,0:T(8,128)(2,1)S(1)} %copy-done.45), kind=kOutput, calls=%fused_computation.318 | convolution fusion | flops 7397703680 | bytes 20840448 | tf_op jit(solution)/shard_map/rf,df->rd/dot_general | solution.py:18
  355.2 15.6 %collective-permute-done.44 = bf16[128,2816]{1,0:T(8,128)(2,1)S(1)} collective-permute-done((bf16[128,2816]{1,0:T(8,128)(2,1)}, bf16[128,2816]{1,0:T(8,128)(2,1)S(1)}, u32[]{:S(2)}, u32[]{:S(2)}) %collective-permute-start.44) | collective-permute-done | bytes 720928 | tf_op jit(solution)/shard_map/ppermute | solution.py:696
  373.6 12.2 %collective-permute-done.46 = bf16[128,2816]{1,0:T(8,128)(2,1)S(1)} collective-permute-done((bf16[128,2816]{1,0:T(8,128)(2,1)}, bf16[128,2816]{1,0:T(8,128)(2,1)S(1)}, u32[]{:S(2)}, u32[]{:S(2)}) %collective-permute-start.46) | collective-permute-done | bytes 720928 | tf_op jit(solution)/shard_map/ppermute | solution.py:696
  386.2 14.3 %collective-permute-done.47 = bf16[128,2816]{1,0:T(8,128)(2,1)S(1)} collective-permute-done((bf16[128,2816]{1,0:T(8,128)(2,1)S(1)}, bf16[128,2816]{1,0:T(8,128)(2,1)S(1)}, u32[]{:S(2)}, u32[]{:S(2)}) %collective-permute-start.47) | collective-permute-done | bytes 720928 | tf_op jit(solution)/shard_map/ppermute | solution.py:696
  406.2 8.2 %collective-permute-start.32 = (bf16[2,80,1024]{2,1,0:T(8,128)(2,1)S(1)}, bf16[2,80,1024]{2,1,0:T(8,128)(2,1)S(1)}, u32[]{:S(2)}, u32[]{:S(2)}) collective-permute-start(bf16[2,80,1024]{2,1,0:T(8,128)(2,1)S(1)} %bitcast.238), channel_id=1, source_target_pairs={{0,1},{1,0},{2,3},{3,2},{4,5},{5,4},{6,7},{7,6},{8,9},{9,8},{10,11... | collective-permute-start | bytes 983048 | tf_op jit(solution)/shard_map/ppermute | solution.py:23
  419.0 13.0 %collective-permute-done.51 = bf16[352,1024]{1,0:T(8,128)(2,1)S(1)} collective-permute-done((bf16[352,1024]{1,0:T(8,128)(2,1)S(1)}, bf16[352,1024]{1,0:T(8,128)(2,1)S(1)}, u32[]{:S(2)}, u32[]{:S(2)}) %collective-permute-start.51) | collective-permute-done | bytes 720928 | tf_op jit(solution)/shard_map/ppermute | solution.py:708
  456.8 15.0 %shard_map.265 = (bf16[2,256,1536]{2,1,0:T(8,128)(2,1)S(1)}, f32[8,512]{1,0:T(8,128)S(1)}) custom-call(s32[2]{0:T(128)S(1)} %bitcast.206, f32[8,512]{1,0:T(8,128)S(1)} %pad_maximum_fusion.16.line_ref, bf16[2,256,1536]{2,1,0:T(8,128)(2,1)S(1)} %copy-done.3, bf16[2,256,512]{2,1,0:T(8,128)(2,1)S(1)} %fusion.26.grad_ref), custom_call_target="tpu_custom_call" | custom-call | tf_op jit(solution)/shard_map/pallas_call | solution.py:148
  481.5 60.4 %shard_map.266 = (f32[32,1024]{1,0:T(8,128)S(1)}, f32[32,1024]{1,0:T(8,128)S(1)}, f32[32,1024]{1,0:T(8,128)S(1)}, f32[32,1024]{1,0:T(8,128)S(1)}, f32[32,128]{1,0:T(8,128)S(1)}, /*index=5*/f32[2,8,512]{2,1,0:T(8,128)S(1)}) custom-call(bf16[2,2,256,1536]{3,2,1,0:T(8,128)(2,1)S(1)} %bitcast.199, bf16[2,2,256,1024]{3,2,1,0:T(8,128)(2,1)S(1)} %bitcast.198, ...), custom_call_target="tpu_custom_call" | custom-call | tf_op jit(solution)/shard_map/pallas_call | solution.py:366
  (352 shorter events, 201.5 us)
Async XLA Ops:
  7.2 105.9 %all-gather.6.cloned.1.call-start = ((), (), s32[]{:S(2)}) async-start(), calls=%async_computation.1 | async-start | bytes 3620864 | tf_op jit(solution)/shard_map/all_gather | solution.py:518
  16.6 132.3 %all-gather.4.cloned.1.call-start = ((), (), s32[]{:S(2)}) async-start(), calls=%async_computation | async-start | bytes 2162688 | tf_op jit(solution)/shard_map/all_gather | solution.py:525
  16.6 68.6 %collective-permute-start.14 = (bf16[352,1024]{1,0:T(8,128)(2,1)}, bf16[352,1024]{1,0:T(8,128)(2,1)}, u32[]{:S(2)}, u32[]{:S(2)}) collective-permute-start(bf16[352,1024]{1,0:T(8,128)(2,1)} %bitcast.276), channel_id=1, source_target_pairs={{0,0},{1,1},{2,2},{3,3},{4,4},{5,5},{6,6},{7,7},{8,16},{9,17},{10,... | collective-permute-start | bytes 2162696 | tf_op jit(solution)/shard_map/ppermute | solution.py:551
  23.5 63.4 %collective-permute-start.15 = (bf16[352,1024]{1,0:T(8,128)(2,1)}, bf16[352,1024]{1,0:T(8,128)(2,1)}, u32[]{:S(2)}, u32[]{:S(2)}) collective-permute-start(bf16[352,1024]{1,0:T(8,128)(2,1)} %bitcast.277), channel_id=1, source_target_pairs={{0,16},{1,17},{2,18},{3,19},{4,20},{5,21},{6,22},{7,23},{8,0},{9,1... | collective-permute-start | bytes 2162696 | tf_op jit(solution)/shard_map/ppermute | solution.py:551
  25.4 82.5 %collective-permute-start.16 = (bf16[352,1024]{1,0:T(8,128)(2,1)}, bf16[352,1024]{1,0:T(8,128)(2,1)}, u32[]{:S(2)}, u32[]{:S(2)}) collective-permute-start(bf16[352,1024]{1,0:T(8,128)(2,1)} %bitcast.278), channel_id=1, source_target_pairs={{0,4},{1,5},{2,6},{3,7},{4,0},{5,1},{6,2},{7,3},{8,20},{9,21},{10,... | collective-permute-start | bytes 2162696 | tf_op jit(solution)/shard_map/ppermute | solution.py:551
  27.2 82.9 %collective-permute-start.17 = (bf16[352,1024]{1,0:T(8,128)(2,1)}, bf16[352,1024]{1,0:T(8,128)(2,1)}, u32[]{:S(2)}, u32[]{:S(2)}) collective-permute-start(bf16[352,1024]{1,0:T(8,128)(2,1)} %bitcast.279), channel_id=1, source_target_pairs={{0,20},{1,21},{2,22},{3,23},{4,16},{5,17},{6,18},{7,19},{8,4},{9,5... | collective-permute-start | bytes 2162696 | tf_op jit(solution)/shard_map/ppermute | solution.py:551
  27.5 43.0 %collective-permute-start.23 = (bf16[2,128,1024]{2,1,0:T(8,128)(2,1)}, bf16[2,128,1024]{2,1,0:T(8,128)(2,1)}, u32[]{:S(2)}, u32[]{:S(2)}) collective-permute-start(bf16[2,128,1024]{2,1,0:T(8,128)(2,1)} %bitcast.228), channel_id=1, source_target_pairs={{0,4},{4,0},{1,5},{5,1},{2,6},{6,2},{3,7},{7,3},{8,12},{12,8},{9,1... | collective-permute-start | bytes 1572872 | tf_op jit(solution)/shard_map/ppermute | solution.py:23
  94.9 65.8 %collective-permute-start.12 = (bf16[128,2816]{1,0:T(8,128)(2,1)}, bf16[128,2816]{1,0:T(8,128)(2,1)}, u32[]{:S(2)}, u32[]{:S(2)}) collective-permute-start(bf16[128,2816]{1,0:T(8,128)(2,1)} %get-tuple-element.172), channel_id=1, source_target_pairs={{0,24},{8,16},{16,8},{24,0},{1,25},{9,17},{17,9},{25,1},{2,26},{10... | collective-permute-start | bytes 2162696 | tf_op jit(solution)/shard_map/ppermute | solution.py:23
  106.1 52.5 %collective-permute-start.9 = (bf16[128,2816]{1,0:T(8,128)(2,1)}, bf16[128,2816]{1,0:T(8,128)(2,1)}, u32[]{:S(2)}, u32[]{:S(2)}) collective-permute-start(bf16[128,2816]{1,0:T(8,128)(2,1)} %collective-permute-done.8), channel_id=1, source_target_pairs={{0,4},{4,0},{1,5},{5,1},{2,6},{6,2},{3,7},{7,3},{8,12},{12,8},{9,1... | collective-permute-start | bytes 2162696 | tf_op jit(solution)/shard_map/ppermute | solution.py:23
  107.9 76.9 %collective-permute-start.11 = (bf16[128,2816]{1,0:T(8,128)(2,1)S(1)}, bf16[128,2816]{1,0:T(8,128)(2,1)}, u32[]{:S(2)}, u32[]{:S(2)}) collective-permute-start(bf16[128,2816]{1,0:T(8,128)(2,1)S(1)} %collective-permute-done.10), channel_id=1, source_target_pairs={{0,4},{4,0},{1,5},{5,1},{2,6},{6,2},{3,7},{7,3},{8,12},{12,8},{9,1... | collective-permute-start | bytes 2162696 | tf_op jit(solution)/shard_map/ppermute | solution.py:23
  160.6 60.3 %collective-permute-start.27 = (bf16[2,80,1024]{2,1,0:T(8,128)(2,1)}, bf16[2,80,1024]{2,1,0:T(8,128)(2,1)}, u32[]{:S(2)}, u32[]{:S(2)}) collective-permute-start(bf16[2,80,1024]{2,1,0:T(8,128)(2,1)} %get-tuple-element.192), channel_id=1, source_target_pairs={{0,1},{1,0},{2,3},{3,2},{4,5},{5,4},{6,7},{7,6},{8,9},{9,8},{10,11... | collective-permute-start | bytes 983048 | tf_op jit(solution)/shard_map/ppermute | solution.py:23
  171.1 49.8 %collective-permute-start.28 = (bf16[2,80,1024]{2,1,0:T(8,128)(2,1)}, bf16[2,80,1024]{2,1,0:T(8,128)(2,1)}, u32[]{:S(2)}, u32[]{:S(2)}) collective-permute-start(bf16[2,80,1024]{2,1,0:T(8,128)(2,1)} %get-tuple-element.191), channel_id=1, source_target_pairs={{0,2},{1,3},{2,0},{3,1},{4,6},{5,7},{6,4},{7,5},{8,10},{9,11},{10,... | collective-permute-start | bytes 983048 | tf_op jit(solution)/shard_map/ppermute | solution.py:23
  184.9 36.0 %collective-permute-start.29 = (bf16[2,80,1024]{2,1,0:T(8,128)(2,1)}, bf16[2,80,1024]{2,1,0:T(8,128)(2,1)S(1)}, u32[]{:S(2)}, u32[]{:S(2)}) collective-permute-start(bf16[2,80,1024]{2,1,0:T(8,128)(2,1)} %get-tuple-element.190), channel_id=1, source_target_pairs={{0,3},{1,2},{2,1},{3,0},{4,7},{5,6},{6,5},{7,4},{8,11},{9,10},{10,... | collective-permute-start | bytes 983048 | tf_op jit(solution)/shard_map/ppermute | solution.py:23
  336.1 34.7 %collective-permute-start.44 = (bf16[128,2816]{1,0:T(8,128)(2,1)}, bf16[128,2816]{1,0:T(8,128)(2,1)S(1)}, u32[]{:S(2)}, u32[]{:S(2)}) collective-permute-start(bf16[128,2816]{1,0:T(8,128)(2,1)} %get-tuple-element.156), channel_id=1, source_target_pairs={{0,28},{1,29},{2,30},{3,31},{4,24},{5,25},{6,26},{7,27},{8,20},{9,... | collective-permute-start | bytes 2162696 | tf_op jit(solution)/shard_map/ppermute | solution.py:696
  338.4 34.3 %collective-permute-start.45 = (bf16[128,2816]{1,0:T(8,128)(2,1)}, bf16[128,2816]{1,0:T(8,128)(2,1)S(1)}, u32[]{:S(2)}, u32[]{:S(2)}) collective-permute-start(bf16[128,2816]{1,0:T(8,128)(2,1)} %get-tuple-element.153), channel_id=1, source_target_pairs={{0,4},{1,5},{2,6},{3,7},{4,0},{5,1},{6,2},{7,3},{8,12},{9,13},{10,... | collective-permute-start | bytes 2162696 | tf_op jit(solution)/shard_map/ppermute | solution.py:696
  340.9 44.9 %collective-permute-start.46 = (bf16[128,2816]{1,0:T(8,128)(2,1)}, bf16[128,2816]{1,0:T(8,128)(2,1)S(1)}, u32[]{:S(2)}, u32[]{:S(2)}) collective-permute-start(bf16[128,2816]{1,0:T(8,128)(2,1)} %get-tuple-element.155), channel_id=1, source_target_pairs={{0,16},{1,17},{2,18},{3,19},{4,20},{5,21},{6,22},{7,23},{8,24},{9,... | collective-permute-start | bytes 2162696 | tf_op jit(solution)/shard_map/ppermute | solution.py:696
  341.5 59.1 %collective-permute-start.47 = (bf16[128,2816]{1,0:T(8,128)(2,1)S(1)}, bf16[128,2816]{1,0:T(8,128)(2,1)S(1)}, u32[]{:S(2)}, u32[]{:S(2)}) collective-permute-start(bf16[128,2816]{1,0:T(8,128)(2,1)S(1)} %get-tuple-element.154), channel_id=1, source_target_pairs={{0,20},{1,21},{2,22},{3,23},{4,16},{5,17},{6,18},{7,19},{8,28},{9,... | collective-permute-start | bytes 2162696 | tf_op jit(solution)/shard_map/ppermute | solution.py:696
  354.5 60.0 %collective-permute-start.48 = (bf16[352,1024]{1,0:T(8,128)(2,1)S(1)}, bf16[352,1024]{1,0:T(8,128)(2,1)S(1)}, u32[]{:S(2)}, u32[]{:S(2)}) collective-permute-start(bf16[352,1024]{1,0:T(8,128)(2,1)S(1)} %get-tuple-element.160), channel_id=1, source_target_pairs={{0,0},{1,1},{2,2},{3,3},{4,4},{5,5},{6,6},{7,7},{16,8},{17,9},{18,... | collective-permute-start | bytes 2162696 | tf_op jit(solution)/shard_map/ppermute | solution.py:708
  370.8 45.7 %collective-permute-start.49 = (bf16[352,1024]{1,0:T(8,128)(2,1)S(1)}, bf16[352,1024]{1,0:T(8,128)(2,1)S(1)}, u32[]{:S(2)}, u32[]{:S(2)}) collective-permute-start(bf16[352,1024]{1,0:T(8,128)(2,1)S(1)} %get-tuple-element.163), channel_id=1, source_target_pairs={{16,0},{17,1},{18,2},{19,3},{20,4},{21,5},{22,6},{23,7},{0,8},{1,9... | collective-permute-start | bytes 2162696 | tf_op jit(solution)/shard_map/ppermute | solution.py:708
  372.7 46.3 %collective-permute-start.50 = (bf16[352,1024]{1,0:T(8,128)(2,1)S(1)}, bf16[352,1024]{1,0:T(8,128)(2,1)S(1)}, u32[]{:S(2)}, u32[]{:S(2)}) collective-permute-start(bf16[352,1024]{1,0:T(8,128)(2,1)S(1)} %get-tuple-element.162), channel_id=1, source_target_pairs={{4,0},{5,1},{6,2},{7,3},{0,4},{1,5},{2,6},{3,7},{20,8},{21,9},{22,... | collective-permute-start | bytes 2162696 | tf_op jit(solution)/shard_map/ppermute | solution.py:708
  385.8 46.2 %collective-permute-start.51 = (bf16[352,1024]{1,0:T(8,128)(2,1)S(1)}, bf16[352,1024]{1,0:T(8,128)(2,1)S(1)}, u32[]{:S(2)}, u32[]{:S(2)}) collective-permute-start(bf16[352,1024]{1,0:T(8,128)(2,1)S(1)} %get-tuple-element.161), channel_id=1, source_target_pairs={{20,0},{21,1},{22,2},{23,3},{16,4},{17,5},{18,6},{19,7},{4,8},{5,9... | collective-permute-start | bytes 2162696 | tf_op jit(solution)/shard_map/ppermute | solution.py:708
  406.2 27.4 %collective-permute-start.32 = (bf16[2,80,1024]{2,1,0:T(8,128)(2,1)S(1)}, bf16[2,80,1024]{2,1,0:T(8,128)(2,1)S(1)}, u32[]{:S(2)}, u32[]{:S(2)}) collective-permute-start(bf16[2,80,1024]{2,1,0:T(8,128)(2,1)S(1)} %bitcast.238), channel_id=1, source_target_pairs={{0,1},{1,0},{2,3},{3,2},{4,5},{5,4},{6,7},{7,6},{8,9},{9,8},{10,11... | collective-permute-start | bytes 983048 | tf_op jit(solution)/shard_map/ppermute | solution.py:23
  448.3 98.0 %collective-permute-start.38 = (bf16[2,128,1024]{2,1,0:T(8,128)(2,1)}, bf16[2,128,1024]{2,1,0:T(8,128)(2,1)}, u32[]{:S(2)}, u32[]{:S(2)}) collective-permute-start(bf16[2,128,1024]{2,1,0:T(8,128)(2,1)} %get-tuple-element.121), channel_id=1, source_target_pairs={{0,4},{4,0},{1,5},{5,1},{2,6},{6,2},{3,7},{7,3},{8,12},{12,8},{9,1... | collective-permute-start | bytes 1572872 | tf_op jit(solution)/shard_map/ppermute | solution.py:23
  474.7 69.8 %collective-permute-start.40 = (bf16[2,128,1024]{2,1,0:T(8,128)(2,1)}, bf16[2,128,1024]{2,1,0:T(8,128)(2,1)}, u32[]{:S(2)}, u32[]{:S(2)}) collective-permute-start(bf16[2,128,1024]{2,1,0:T(8,128)(2,1)} %dynamic-slice_convert_fusion.4), channel_id=1, source_target_pairs={{0,4},{4,0},{1,5},{5,1},{2,6},{6,2},{3,7},{7,3},{8,12},{12,8},{9,1... | collective-permute-start | bytes 1572872 | tf_op jit(solution)/shard_map/ppermute | solution.py:23
  (78 other events, 1066.1 us)
Sparse Core Ops, SparseCore 0:
  16.7 54.7 all-gather.5
  74.4 60.4 all-gather.3

commit v2 on v1

--- a/solution.py
+++ b/solution.py
@@ -452,7 +452,7 @@
     return pairs
 
 
-def body(
+def plain_body(
     activations,
     cotangent,
     dealing,
@@ -489,12 +489,6 @@
     weight_rows = w_query.shape[0]
     plane = dp_count * ctx_count
     plane_index = dp_index * ctx_count + ctx_index
-    tuned = (
-        (dp_count, ctx_count, expert_count) == (4, 2, 4)
-        and weight_rows % 16 == 0
-        and own_width % 128 == 0
-        and width % own_width == 0
-    )
     act = activations[:, 0]
     cot = cotangent[:, 0]
     deal = dealing[:, 0]
@@ -761,26 +755,13 @@
     grad_input = (to_positions(hidden_low) + rows_back).astype(BF16)[:, None]
     output = to_positions(final).astype(BF16)[:, None]
 
-    if tuned:
-        small = jnp.concatenate(
-            [router_total, second_total[:, None], first_total[:, None]], axis=1
-        )
-        small = jnp.pad(small, ((0, 0), (0, 128 - small.shape[1]))).astype(BF16)
-        grad_query, grad_key, grad_value, grad_out, small_sum, diag_all = reduce_dense(
-            qkv_total.astype(BF16), out_total.astype(BF16), small, diagonals, own_width
-        )
-        grad_router = small_sum[:, :experts]
-        grad_second = small_sum[:, experts]
-        grad_first = small_sum[:, experts + 1]
-        diag_all = diag_all.reshape((head_count, -1))
-    else:
-        sums = plain_sums(
-            qkv_total, out_total, router_total, first_total, second_total, own_width
-        )
-        grad_query, grad_key, grad_value, grad_out, grad_router, grad_first, grad_second = sums
-        diag_all = lax.all_gather(
-            lax.psum(diagonals, ("dp", "experts")), "context", axis=0, tiled=True
-        )
+    sums = plain_sums(
+        qkv_total, out_total, router_total, first_total, second_total, own_width
+    )
+    grad_query, grad_key, grad_value, grad_out, grad_router, grad_first, grad_second = sums
+    diag_all = lax.all_gather(
+        lax.psum(diagonals, ("dp", "experts")), "context", axis=0, tiled=True
+    )
     offsets = jnp.concatenate([diag_all[:, :1], diag_all[:, : seq : -1]], axis=1)
     grad_table = jnp.einsum(
         "hs,sb->bh", offsets, bucket_hot.astype(F32), precision=lax.Precision.HIGHEST
@@ -802,6 +783,803 @@
     )
 
 
+class Wires:
+    def __init__(self, sends, receives, homes):
+        self.sends, self.receives, self.homes = sends, receives, homes
+        self.used, self.used_home = 0, 0
+
+    def take(self):
+        self.used += 1
+        return self.used - 1
+
+    def copy(self, source, place, peer, index):
+        return remote(source, place, self.sends.at[index], self.receives.at[index], peer)
+
+    def home(self, source, place):
+        copy = pltpu.make_async_copy(source, place, self.homes.at[self.used_home])
+        self.used_home += 1
+        return copy
+
+
+class Spread:
+    def __init__(self, wires, buf, ctx_axis):
+        self.wires, self.buf = wires, buf
+        dp, ctx, exp = (lax.axis_index(name) for name in ALL)
+        self.high, self.low, self.exp = dp // 2, dp % 2, exp
+        self.last = lax.axis_size("experts") - 1
+        self.core_peer = (flip(dp, 1), ctx, exp)
+        self.x_peer = (flip(dp, 2), ctx, exp)
+        self.up_peer = (dp, ctx, jnp.minimum(exp + 1, self.last))
+        self.down_peer = (dp, ctx, jnp.maximum(exp - 1, 0))
+        self.labels = [(0, 0)] + [(h, d) for h in range(1, self.last + 1) for d in (1, -1)]
+        self.z_wire, self.x_wire, self.own_wire, self.far_wire = (
+            {label: wires.take() for label in self.labels} for _ in range(4)
+        )
+
+    def block(self, label):
+        hop, way = label
+        return jnp.clip(self.exp - hop * way, 0, self.last) if hop else self.exp
+
+    def when(self, label):
+        hop, way = label
+        if hop == 0:
+            return lambda f: f()
+        here = self.exp - hop * way
+        return pl.when((here >= 0) & (here <= self.last))
+
+    def can_send(self, label, act):
+        hop, way = label
+        held = self.exp - (hop - 1) * way
+        ahead = self.exp + way
+        pl.when((held >= 0) & (held <= self.last) & (ahead >= 0) & (ahead <= self.last))(act)
+
+    def z_copy(self, label):
+        hop, way = label
+        held = jnp.clip(self.exp - (hop - 1) * way, 0, self.last)
+        part = self.buf.at[self.high, self.low, :, held]
+        peer = self.up_peer if way == 1 else self.down_peer
+        return self.wires.copy(part, part, peer, self.z_wire[label])
+
+    def part_copy(self, label, high, wire, peer):
+        part = self.buf.at[high, self.low, :, self.block(label)]
+        return self.wires.copy(part, part, peer, wire[label])
+
+    def x_copy(self, label):
+        return self.part_copy(label, self.high, self.x_wire, self.x_peer)
+
+    def own_copy(self, label):
+        return self.part_copy(label, self.high, self.own_wire, self.core_peer)
+
+    def far_copy(self, label):
+        return self.part_copy(label, 1 - self.high, self.far_wire, self.core_peer)
+
+    def spread(self, label):
+        self.x_copy(label).start()
+        self.own_copy(label).start()
+
+    def begin(self):
+        for way in (1, -1):
+            self.can_send((1, way), lambda way=way: self.z_copy((1, way)).start())
+        self.spread((0, 0))
+
+    def hop(self, hop):
+        for way in (1, -1):
+            label = (hop, way)
+
+            @self.when(label)
+            def _(label=label):
+                part = self.buf.at[self.high, self.low, :, self.block(label)]
+                self.wires.copy(part, part, self.up_peer, self.z_wire[label]).wait_recv()
+
+            if hop < self.last:
+                nxt = (hop + 1, way)
+                self.can_send(nxt, lambda nxt=nxt: self.z_copy(nxt).start())
+
+            @self.when(label)
+            def _(label=label):
+                self.spread(label)
+
+        for label in self.labels:
+            if label[0] == hop - 1:
+                self.pass_far(label)
+
+    def pass_far(self, label):
+        @self.when(label)
+        def _():
+            self.x_copy(label).wait_recv()
+            self.far_copy(label).start()
+
+    def end(self):
+        for label in self.labels:
+            if label[0] == self.last:
+                self.pass_far(label)
+        for label in self.labels:
+
+            @self.when(label)
+            def _(label=label):
+                self.own_copy(label).wait_recv()
+                self.far_copy(label).wait_recv()
+
+    def drain(self):
+        for label in self.labels:
+            if label[0]:
+                self.can_send(label, lambda label=label: self.z_copy(label).wait_send())
+
+            @self.when(label)
+            def _(label=label):
+                self.x_copy(label).wait_send()
+                self.own_copy(label).wait_send()
+                self.far_copy(label).wait_send()
+
+
+def front_kernel(
+    sizes,
+    act_ref,
+    cot_ref,
+    deal_ref,
+    length_ref,
+    route_ref,
+    line_ref,
+    query_ref,
+    key_ref,
+    value_ref,
+    out_ref,
+    extra_ref,
+    gate_ref,
+    up_ref,
+    down_ref,
+    dense,
+    out_w,
+    act_all,
+    normed_ref,
+    qkv_ref,
+    mixed,
+    hidden_ref,
+    logit_ref,
+    cot_rows_ref,
+    all_x,
+    all_u,
+    all_p,
+    gate_up,
+    down,
+    cot_all,
+    mixed_own,
+    mixed_sent,
+    sent_x,
+    sent_u,
+    sent_p,
+    sends,
+    receives,
+    homes,
+):
+    heads, head_size, experts, capacity, slots = sizes
+    micro, rows_dev, width = act_ref.shape
+    own_width = heads * head_size
+    half = gate_ref.shape[1] // 2
+    dp, ctx, exp = (lax.axis_index(name) for name in ALL)
+    high, low = dp // 2, dp % 2
+    block = dp * 2 + ctx
+    core_peer, x_peer, x_core = ((flip(dp, 1), ctx, exp), (flip(dp, 2), ctx, exp), (3 - dp, ctx, exp))
+    x_core = (flip(flip(dp, 2), 1), ctx, exp)
+    y_peer, y_core = (dp, 1 - ctx, exp), (flip(dp, 1), 1 - ctx, exp)
+    z_peers = [None] + [(dp, ctx, flip(exp, 1)), (dp, ctx, flip(exp, 2)), (dp, ctx, 3 - exp)]
+    z_index = [exp, flip(exp, 1), flip(exp, 2), 3 - exp]
+    greet([core_peer, x_peer, x_core, y_peer, y_core] + z_peers[1:])
+    wires = Wires(sends, receives, homes)
+    drains = []
+    home_copies = []
+
+    def send(source, place, peer):
+        copy = wires.copy(source, place, peer, wires.take())
+        copy.start()
+        drains.append(copy)
+        return copy
+
+    def multiple(index, size):
+        return pl.ds(pl.multiple_of(index * size, size), size)
+
+    mine, other = multiple(ctx, own_width), multiple(1 - ctx, own_width)
+    first = []
+    for i, ref in enumerate((query_ref, key_ref, value_ref)):
+        place = dense.at[high, low, ctx, exp, :, i * own_width : (i + 1) * own_width]
+        first.append(send(ref.at[:, other], place, y_peer))
+    first.append(send(extra_ref, dense.at[high, low, ctx, exp, :, 3 * own_width :], y_peer))
+    out_first = send(out_ref, out_w.at[high, low, ctx, exp], y_peer)
+    here = multiple(ctx, rows_dev)
+    act_first = send(act_ref, act_all.at[:, here], y_peer)
+    for i, ref in enumerate((query_ref, key_ref, value_ref)):
+        dense[high, low, ctx, exp, :, i * own_width : (i + 1) * own_width] = ref[:, mine]
+    dense[high, low, ctx, exp, :, 3 * own_width :] = extra_ref[...]
+    out_w[high, low, ctx, exp] = out_ref[...]
+    act_all[:, here, :] = act_ref[...]
+    cot_all[:, here, :] = cot_ref[...]
+
+    spread = Spread(wires, dense, 2)
+    spread_out = Spread(wires, out_w, 2)
+    for copy in first:
+        copy.wait_recv()
+    spread.begin()
+    cot_first = send(cot_ref, cot_all.at[:, here], y_peer)
+
+    def gate_sends(core, peer):
+        cols = multiple(core, half)
+        return [
+            send(gate_ref.at[:, cols], gate_up.at[block, :, 0:half], peer),
+            send(up_ref.at[:, cols], gate_up.at[block, :, half:], peer),
+        ]
+
+    for ref, start in ((gate_ref, 0), (up_ref, half)):
+        copy = wires.home(ref.at[:, multiple(low, half)], gate_up.at[block, :, start : start + half])
+        copy.start()
+        home_copies.append(copy)
+
+    spread.hop(1)
+    from_core = gate_sends(1 - low, core_peer)
+    from_x = gate_sends(low, x_peer)
+    from_y = gate_sends(low, y_peer)
+    from_x_core = gate_sends(1 - low, x_core)
+    from_y_core = gate_sends(1 - low, y_core)
+
+    own_down = low * 2 + ctx
+    home_down = wires.home(down_ref, down.at[own_down])
+    down_wire = {name: wires.take() for name in ("core", "x", "xc", "y", "yc", "rx", "ry")}
+    at_home = low == high
+
+    def down_copy(name, peer, source=None):
+        source = down_ref if source is None else source
+        return wires.copy(source, down.at[own_down], peer, down_wire[name])
+
+    down_sends = [
+        ("core", core_peer, False),
+        ("x", x_peer, True),
+        ("xc", x_core, False),
+        ("y", y_peer, True),
+        ("yc", y_core, False),
+    ]
+
+    def down_start():
+        @pl.when(at_home)
+        def _():
+            home_down.start()
+
+        for name, peer, straight in down_sends:
+            pl.when(at_home == straight)(lambda name=name, peer=peer: down_copy(name, peer).start())
+
+    lane = lax.broadcasted_iota(jnp.int32, (rows_dev, 128), 1)
+    lane_f = lane.astype(F32)
+    row_id = lax.broadcasted_iota(jnp.int32, (rows_dev, rows_dev), 0)
+    col_id = lax.broadcasted_iota(jnp.int32, (rows_dev, rows_dev), 1)
+    before = (row_id > col_id).astype(BF16)
+    seq = deal_ref.shape[1]
+    seq_lane = lax.broadcasted_iota(jnp.int32, (rows_dev, seq), 1)
+
+    def hot(m, k):
+        index = ctx if k == 0 else 1 - ctx
+        return (deal_ref[m, multiple(index, rows_dev), :] == seq_lane).astype(BF16)
+
+    def live_slots(m):
+        return deal_ref[m, here, :] < length_ref[m]
+
+    def ranks(m):
+        live = live_slots(m)
+        hots = [(route_ref[m, :, j : j + 1] == lane) for j in range(2)]
+        used = jnp.where((hots[0] | hots[1]) & live, 1.0, 0.0).astype(BF16)
+        earlier = jnp.dot(before, used, preferred_element_type=F32)
+        found = []
+        for j in range(2):
+            rank = jnp.sum(jnp.where(hots[j], earlier, 0.0), axis=1, keepdims=True)
+            found.append(jnp.where(live & (rank < capacity), rank, -1.0))
+        return found
+
+    def picks(m, k, rank):
+        return [
+            (route_ref[m, :, j : j + 1] == z_index[k]) & (rank[j] == lane_f) for j in range(2)
+        ]
+
+    def as_rows(pick, value):
+        chosen = lax.dot_general(
+            pick, value, (((0,), (0,)), ((), ())), preferred_element_type=F32
+        )
+        return chosen[:slots].astype(BF16)
+
+    spread.hop(2)
+    rank_of = [ranks(m) for m in range(micro)]
+    act_first.wait_recv()
+    spread.hop(3)
+    cot_first.wait_recv()
+    pick_of = {}
+    for m in range(micro):
+        hot_mine = hot(m, 0)
+        cot_rows = jnp.dot(hot_mine, cot_all[m], preferred_element_type=F32).astype(BF16)
+        cot_rows_ref[m] = cot_rows
+        for k in range(experts):
+            pick = picks(m, k, rank_of[m])
+            pick_any = jnp.where(pick[0] | pick[1], 1.0, 0.0).astype(BF16)
+            rows = as_rows(pick_any, cot_rows)
+            if k == 0:
+                all_u[0, 0, m] = rows
+            else:
+                sent_u[k - 1, m] = rows
+    out_first.wait_recv()
+    spread.end()
+    spread_out.begin()
+
+    extras = dense[:, :, :, :, :, 3 * own_width :].reshape(width, 128).astype(F32)
+    turned = extras.T
+    gain_one, gain_two = turned[experts : experts + 1], turned[experts + 1 : experts + 2]
+    for m in range(micro):
+        rows = act_all[m].astype(F32)
+        inverse = lax.rsqrt(jnp.mean(rows * rows, axis=-1, keepdims=True) + epsilon)
+        normed_ref[m] = (rows * inverse * gain_one).astype(BF16)
+    for i in range(3):
+        weight = dense[:, :, :, :, :, i * own_width : (i + 1) * own_width].reshape(width, own_width)
+        for m in range(micro):
+            qkv_ref[m, :, i * own_width : (i + 1) * own_width] = jnp.dot(
+                normed_ref[m], weight, preferred_element_type=F32
+            ).astype(BF16)
+    spread_out.hop(1)
+    down_start()
+
+    scale = head_size ** (-0.5)
+    mixed_first = []
+    u_first, u_core = {}, []
+    for m in range(micro):
+        length = length_ref[m]
+        for head in range(heads):
+            at = [
+                slice(part * own_width + head * head_size, part * own_width + (head + 1) * head_size)
+                for part in range(3)
+            ]
+            scores = masked_scores(
+                qkv_ref[m, :, at[0]], qkv_ref[m, :, at[1]], line_ref[head : head + 1, :], length, scale
+            )
+            probs = soft(scores).astype(BF16)
+            mixed_own[:, at[0]] = jnp.dot(
+                probs, qkv_ref[m, :, at[2]], preferred_element_type=F32
+            ).astype(BF16)
+        own = mixed_own[...]
+        mixed_sent[m] = jnp.dot(hot(m, 1), own, preferred_element_type=F32).astype(BF16)
+        mixed_first.append(send(mixed_sent.at[m], mixed.at[m, :, mine], y_peer))
+        mixed[m, :, mine] = jnp.dot(hot(m, 0), own, preferred_element_type=F32).astype(BF16)
+        spread_out.hop(2 + m)
+        for k in range(1, experts):
+            u_first[k, m] = send(sent_u.at[k - 1, m], all_u.at[0, k, m], z_peers[k])
+        u_core.append(send(all_u.at[0, 0, m], all_u.at[1, 0, m], core_peer))
+    spread_out.end()
+
+    for copy in from_x:
+        copy.wait_recv()
+    x_block = flip(dp, 2) * 2 + ctx
+    relay_y = send(gate_up.at[x_block], gate_up.at[x_block], y_peer)
+    for copy in from_y_core:
+        copy.wait_recv()
+    y_block = flip(dp, 1) * 2 + 1 - ctx
+    relay_x = send(gate_up.at[y_block], gate_up.at[y_block], x_peer)
+
+    router_w = dense[:, :, :, :, :, 3 * own_width :].reshape(width, 128)
+    x_first, p_first, core_copies = {}, {}, []
+    for m in range(micro):
+        mixed_first[m].wait_recv()
+        branch = jnp.dot(
+            mixed[m], out_w[...].reshape(width, width), preferred_element_type=F32
+        )
+        rows_in = jnp.dot(hot(m, 0), act_all[m], preferred_element_type=F32)
+        live = live_slots(m)
+        hidden = rows_in + jnp.where(live, branch, 0.0)
+        hidden_ref[m] = hidden
+        inverse = lax.rsqrt(jnp.mean(hidden * hidden, axis=-1, keepdims=True) + epsilon)
+        normed_two = (hidden * inverse * gain_two).astype(BF16)
+        logits = jnp.dot(normed_two, router_w, preferred_element_type=F32)
+        logit_ref[m] = logits
+        chosen = [
+            jnp.sum(jnp.where(route_ref[m, :, j : j + 1] == lane, logits, 0.0), axis=1, keepdims=True)
+            for j in range(2)
+        ]
+        top = jnp.maximum(chosen[0], chosen[1])
+        raised = [jnp.exp(c - top) for c in chosen]
+        total = raised[0] + raised[1]
+        gates = [r / total for r in raised]
+        for k in range(experts):
+            pick = picks(m, k, rank_of[m])
+            pick_any = jnp.where(pick[0] | pick[1], 1.0, 0.0).astype(BF16)
+            rows = as_rows(pick_any, normed_two)
+            weights = jnp.sum(
+                jnp.where(pick[0], gates[0], 0.0) + jnp.where(pick[1], gates[1], 0.0),
+                axis=0,
+                keepdims=True,
+            )
+            weights = jnp.broadcast_to(weights, (8, 128))
+            if k == 0:
+                all_x[0, 0, m] = rows
+                all_p[0, 0, m] = weights
+                core_copies.append(send(all_x.at[0, 0, m], all_x.at[1, 0, m], core_peer))
+                core_copies.append(send(all_p.at[0, 0, m], all_p.at[1, 0, m], core_peer))
+            else:
+                sent_x[k - 1, m] = rows
+                sent_p[k - 1, m] = weights
+                x_first[k, m] = send(sent_x.at[k - 1, m], all_x.at[0, k, m], z_peers[k])
+                p_first[k, m] = send(sent_p.at[k - 1, m], all_p.at[0, k, m], z_peers[k])
+
+    away = jnp.logical_not(at_home)
+    rx_place = low * 2 + 1 - ctx
+    ry_place = (1 - low) * 2 + ctx
+
+    @pl.when(at_home)
+    def _():
+        down_copy("y", y_peer).wait_recv()
+        wires.copy(down.at[rx_place], down.at[rx_place], x_peer, down_wire["rx"]).start()
+
+    @pl.when(away)
+    def _():
+        down_copy("xc", x_core).wait_recv()
+        wires.copy(down.at[ry_place], down.at[ry_place], y_peer, down_wire["ry"]).start()
+
+    for m in range(micro):
+        for k in range(1, experts):
+            u_first[k, m].wait_recv()
+            u_core.append(send(all_u.at[0, k, m], all_u.at[1, k, m], core_peer))
+    for m in range(micro):
+        for k in range(1, experts):
+            x_first[k, m].wait_recv()
+            core_copies.append(send(all_x.at[0, k, m], all_x.at[1, k, m], core_peer))
+            p_first[k, m].wait_recv()
+            core_copies.append(send(all_p.at[0, k, m], all_p.at[1, k, m], core_peer))
+
+    for copy in from_core + from_y + from_x_core + [relay_x, relay_y] + u_core + core_copies:
+        copy.wait_recv()
+
+    @pl.when(at_home)
+    def _():
+        for name in ("core", "yc"):
+            down_copy(name, core_peer).wait_recv()
+        home_down.wait()
+        down_copy("rx", x_peer).wait_send()
+
+    @pl.when(away)
+    def _():
+        for name in ("x", "rx", "ry"):
+            down_copy(name, core_peer).wait_recv()
+        down_copy("ry", y_peer).wait_send()
+
+    for name, peer, straight in down_sends:
+        pl.when(at_home == straight)(lambda name=name, peer=peer: down_copy(name, peer).wait_send())
+    for copy in home_copies:
+        copy.wait()
+    for copy in drains:
+        copy.wait_send()
+    spread.drain()
+    spread_out.drain()
+
+
+def front(sizes, act, cot, deal, length, route, lines, weights, extras, w_gate, w_up, w_down):
+    heads, head_size, experts, capacity, slots = sizes
+    micro, rows_dev, width = act.shape
+    own_width = heads * head_size
+    per_row = weights[0].shape[0]
+    seq = deal.shape[1]
+    half = w_gate.shape[1] // 2
+    in_vmem, in_hbm = pl.BlockSpec(memory_space=pltpu.VMEM), pl.BlockSpec(memory_space=pltpu.HBM)
+    wide = 3 * own_width + 128
+    outs = [
+        ((2, 2, 2, 4, per_row, wide), BF16),
+        ((2, 2, 2, 4, per_row, width), BF16),
+        ((micro, seq, width), BF16),
+        ((micro, seq, width), BF16),
+        ((micro, seq, 3 * own_width), BF16),
+        ((micro, rows_dev, width), BF16),
+        ((micro, rows_dev, width), F32),
+        ((micro, rows_dev, 128), F32),
+        ((micro, rows_dev, width), BF16),
+        ((2, experts, micro, slots, width), BF16),
+        ((2, experts, micro, slots, width), BF16),
+        ((2, experts, micro, 8, 128), F32),
+        ((8,) + (w_gate.shape[0], 2 * half), BF16),
+        ((4,) + w_down.shape, BF16),
+    ]
+    return pl.pallas_call(
+        functools.partial(front_kernel, sizes),
+        out_shape=tuple(jax.ShapeDtypeStruct(*out) for out in outs),
+        in_specs=[in_vmem] * 3 + [pl.BlockSpec(memory_space=pltpu.SMEM)] + [in_vmem] * 7 + [in_hbm] * 3,
+        out_specs=(in_vmem,) * 12 + (in_hbm,) * 2,
+        scratch_shapes=[
+            pltpu.VMEM((micro, seq, width), BF16),
+            pltpu.VMEM((seq, own_width), BF16),
+            pltpu.VMEM((micro, rows_dev, own_width), BF16),
+            pltpu.VMEM((experts - 1, micro, slots, width), BF16),
+            pltpu.VMEM((experts - 1, micro, slots, width), BF16),
+            pltpu.VMEM((experts - 1, micro, 8, 128), F32),
+            pltpu.SemaphoreType.DMA((160,)),
+            pltpu.SemaphoreType.DMA((160,)),
+            pltpu.SemaphoreType.DMA((4,)),
+        ],
+        compiler_params=pltpu.CompilerParams(
+            collective_id=1, has_side_effects=True, vmem_limit_bytes=56 * 2**20
+        ),
+    )(act, cot, deal[:, :, None], length, route, lines, *weights, extras, w_gate, w_up, w_down)
+
+
+def tuned_body(
+    activations,
+    cotangent,
+    dealing,
+    lengths,
+    routes,
+    buckets,
+    w_query,
+    w_key,
+    w_value,
+    w_out,
+    w_router,
+    norm_first,
+    norm_second,
+    bias_table,
+    w_gate,
+    w_up,
+    w_down,
+):
+    micro, _, rows_dev, width = activations.shape
+    seq = dealing.shape[2]
+    bucket_count, head_count = bias_table.shape
+    dp_count, ctx_count, expert_count = (lax.axis_size(name) for name in ALL)
+    dp_index, ctx_index, expert_index = (lax.axis_index(name) for name in ALL)
+    high, low = dp_index // 2, dp_index % 2
+    heads = head_count // ctx_count
+    head_size = width // head_count
+    own_width = heads * head_size
+    experts = w_router.shape[1]
+    top_count = routes.shape[3]
+    capacity = (5 * rows_dev * top_count + 4 * experts - 1) // (4 * experts)
+    slots = -(-capacity // 16) * 16
+    half_ff = w_gate.shape[2] // 2
+    down_rows = w_down.shape[1]
+    plane = dp_count * ctx_count
+    plane_index = dp_index * ctx_count + ctx_index
+    act = activations[:, 0]
+    cot = cotangent[:, 0]
+    deal = dealing[:, 0]
+    length = lengths[:, 0]
+    route = routes[:, 0]
+    extras = jnp.concatenate([w_router, norm_first[:, None], norm_second[:, None]], axis=1)
+    extras = jnp.pad(extras, ((0, 0), (0, 128 - extras.shape[1])))
+    bucket_hot = (buckets[:, None] == jnp.arange(bucket_count)[None, :]).astype(BF16)
+    own_table = lax.dynamic_slice_in_dim(bias_table, ctx_index * heads, heads, axis=1)
+    lookup = dot_f32("sb,bh->hs", bucket_hot, own_table)
+    lines = jnp.concatenate(
+        [lookup[:, :1], jnp.zeros((heads, seq), F32), lookup[:, :0:-1]], axis=1
+    )
+    (
+        dense,
+        out_w,
+        act_all,
+        normed,
+        qkv,
+        mixed,
+        hidden,
+        logits,
+        cot_low,
+        all_x,
+        all_u,
+        all_p,
+        gate_up_w,
+        down_w,
+    ) = front(
+        (heads, head_size, experts, capacity, slots),
+        act,
+        cot,
+        deal,
+        length,
+        route,
+        lines,
+        (w_query, w_key, w_value, w_out),
+        extras,
+        w_gate[0],
+        w_up[0],
+        w_down[0],
+    )
+    dense = dense.reshape(width, -1)
+    qkv_w = dense[:, : 3 * own_width]
+    router_w = dense[:, 3 * own_width : 3 * own_width + experts]
+    gain_one = dense[:, 3 * own_width + experts].astype(F32)
+    gain_two = dense[:, 3 * own_width + experts + 1].astype(F32)
+    out_w = out_w.reshape(width, width)
+    gate_up_w = gate_up_w.reshape(width, 2 * half_ff)
+    down_w = down_w.reshape(half_ff, width)
+    row_count = experts * micro * slots
+
+    all_x = all_x.reshape(2 * row_count, width)
+    own_u = all_u[0].reshape(row_count, width)
+    all_p = all_p[..., 0, :slots].reshape(2 * row_count, 1)
+    all_g = (all_p * all_u.reshape(2 * row_count, width).astype(F32)).astype(BF16)
+    pre_up = dot_f32("rd,df->rf", all_x, gate_up_w)
+    gelu_value, gelu_slope = gelu_parts(pre_up[:, :half_ff])
+    up_part = pre_up[:, half_ff:]
+    activated = (gelu_value * up_part).astype(BF16)
+    act_grad = dot_f32("rd,fd->rf", all_g, down_w)
+    pre_grad = (act_grad * up_part * gelu_slope).astype(BF16)
+    up_grad = (act_grad * gelu_value).astype(BF16)
+    both_grad = jnp.concatenate([pre_grad, up_grad], axis=1)
+    back_part = dot_f32("rf,df->rd", both_grad, gate_up_w)
+    out_part = dot_f32("rf,fd->rd", activated, down_w)
+    out_own = (
+        out_part[:row_count] + swap(out_part[row_count:].astype(BF16), "dp", 1).astype(F32)
+    ).astype(BF16)
+    back_own = (
+        back_part[:row_count] + swap(back_part[row_count:].astype(BF16), "dp", 1).astype(F32)
+    ).astype(BF16)
+    gate_rows = jnp.sum(own_u.astype(F32) * out_own.astype(F32), axis=-1)
+
+    def to_source(value):
+        parts = value.reshape((expert_count, micro, slots) + value.shape[1:])
+        parts = [parts[0]] + [swap(parts[k], "experts", k) for k in range(1, expert_count)]
+        parts = jnp.stack(parts)
+        return jnp.moveaxis(parts, 0, 1).reshape((micro, experts * slots) + value.shape[1:])
+
+    back_rows = to_source(back_own)
+    gate_back = to_source(gate_rows)
+    out_rows = to_source(out_own)
+    gate_up_total = dot_f32("rd,rf->df", all_x, both_grad).astype(BF16)
+    down_total = dot_f32("rf,rd->fd", activated, all_g).astype(BF16)
+
+    gate_up_sums = [0.0, 0.0]
+    for j in range(plane):
+        dp_offset, ctx_offset = j // ctx_count, j % ctx_count
+        block = lax.dynamic_slice_in_dim(
+            gate_up_total, (plane_index ^ j) * (width // plane), width // plane, axis=0
+        )
+        pairs = [
+            (
+                (d * ctx_count + c) * expert_count + e,
+                ((d ^ dp_offset) * ctx_count + (c ^ ctx_offset)) * expert_count + e,
+            )
+            for d in range(dp_count)
+            for c in range(ctx_count)
+            for e in range(expert_count)
+        ]
+        if j:
+            block = lax.ppermute(block, ALL, pairs)
+        gate_up_sums[dp_offset % 2] = gate_up_sums[dp_offset % 2] + block.astype(F32)
+    first_half, second_half = reorder(gate_up_sums, low)
+    grad_gate = jnp.concatenate([first_half[:, :half_ff], second_half[:, :half_ff]], axis=1)
+    grad_up = jnp.concatenate([first_half[:, half_ff:], second_half[:, half_ff:]], axis=1)
+    grad_down = 0.0
+    for ctx_offset in range(ctx_count):
+        for core in range(2):
+            pairs = down_routes(dp_count, ctx_count, expert_count, core, ctx_offset)
+            from_core = jnp.where(low == high, core, 1 - core)
+            place = (from_core * ctx_count + (ctx_index ^ ctx_offset)) * down_rows
+            piece = lax.dynamic_slice_in_dim(down_total, place, down_rows, axis=0)
+            arrived = lax.ppermute(piece, ALL, [(b, a) for a, b in pairs])
+            grad_down = grad_down + arrived.astype(F32)
+
+    position_ids = jnp.arange(seq, dtype=jnp.int32)
+    slot_blocks = [
+        lax.dynamic_slice_in_dim(deal, (ctx_index ^ k) * rows_dev, rows_dev, axis=1)
+        for k in range(ctx_count)
+    ]
+    hot = [
+        (block[:, :, None] == position_ids[None, None, :]).astype(BF16) for block in slot_blocks
+    ]
+    my_positions = ctx_index * rows_dev + jnp.arange(rows_dev, dtype=jnp.int32)
+    hot_mine = [
+        (block[:, :, None] == my_positions[None, None, :]).astype(BF16) for block in slot_blocks
+    ]
+    live = slot_blocks[0] < length[:, None]
+    live_rows = live.astype(F32)[:, :, None]
+    route_hot = (route[..., None] == jnp.arange(experts)).astype(F32)
+    chosen = jnp.sum(route_hot * logits[:, :, None, :experts], axis=3)
+    gate_probs = jax.nn.softmax(chosen, axis=-1)
+    flat_hot = (route_hot * live_rows[..., None]).reshape(micro, rows_dev * top_count, experts)
+    pair_ids = jnp.arange(rows_dev * top_count)
+    before = (pair_ids[:, None] > pair_ids[None, :]).astype(BF16)
+    earlier = dot_f32("ab,mbe->mae", before, flat_hot.astype(BF16))
+    rank = jnp.sum(earlier * flat_hot, axis=2).astype(jnp.int32).reshape(route.shape)
+    kept = live[:, :, None] & (rank < capacity)
+    target = jnp.where(kept, (route ^ expert_index) * slots + rank, -1)
+    place_ids = jnp.arange(experts * slots, dtype=jnp.int32)
+    pick = [(target[:, None, :, j] == place_ids[None, :, None]) for j in range(top_count)]
+    pick_any = functools.reduce(jnp.logical_or, pick).astype(BF16)
+    pick_bf = [p.astype(BF16) for p in pick]
+
+    cot_rows = cot_low.astype(F32)
+    inverse_two = lax.rsqrt(jnp.mean(hidden * hidden, axis=-1, keepdims=True) + epsilon)
+    normed_two = (hidden * inverse_two * gain_two).astype(BF16)
+    pair_out = [dot_f32("mrs,mrd->msd", pick_bf[j], out_rows) for j in range(top_count)]
+    final = hidden + sum(gate_probs[:, :, j, None] * pair_out[j] for j in range(top_count))
+    final = final.astype(BF16)
+    gate_grad = jnp.stack(
+        [
+            jnp.sum(jnp.where(pick[j], gate_back[:, :, None], 0.0), axis=1)
+            for j in range(top_count)
+        ],
+        axis=-1,
+    )
+    chosen_grad = gate_probs * (
+        gate_grad - jnp.sum(gate_probs * gate_grad, axis=-1, keepdims=True)
+    )
+    logit_grad = jnp.sum(route_hot * chosen_grad[..., None], axis=2).astype(BF16)
+    normed_grad = dot_f32("mrs,mrd->msd", pick_any, back_rows) + dot_f32(
+        "mse,de->msd", logit_grad, router_w
+    )
+    router_total = dot_f32("msd,mse->de", normed_two, logit_grad)
+    hidden_norm_grad, second_total = norm_pull(hidden, inverse_two, gain_two, normed_grad)
+    hidden_grad = cot_rows + hidden_norm_grad
+    branch_grad = (hidden_grad * live_rows).astype(BF16)
+    hidden_low = hidden_grad.astype(BF16)
+    out_total = dot_f32("msi,mso->io", mixed, branch_grad)
+    mixed_grad = dot_f32("mso,io->msi", branch_grad, out_w).astype(BF16)
+    grad_parts = reorder(jnp.split(mixed_grad, ctx_count, axis=-1), ctx_index)
+    grad_parts = [grad_parts[0]] + [
+        swap(grad_parts[k], "context", k) for k in range(1, ctx_count)
+    ]
+    mixed_back = sum(
+        dot_f32("msp,msw->mpw", hot[k], grad_parts[k]) for k in range(ctx_count)
+    ).astype(BF16)
+    qkv_grad, diagonals = attend_back(qkv, mixed_back, lines, length, heads)
+    qkv_total = dot_f32("mpd,mpw->dw", normed, qkv_grad)
+    first_part = dot_f32("mpw,dw->mpd", qkv_grad, qkv_w)
+    rows_all = act_all.astype(F32)
+    inverse_one = lax.rsqrt(jnp.mean(rows_all * rows_all, axis=-1, keepdims=True) + epsilon)
+    first_total = jnp.sum(first_part * rows_all * inverse_one, axis=(0, 1))
+    blocks = [
+        lax.dynamic_slice_in_dim(first_part, (ctx_index ^ k) * rows_dev, rows_dev, axis=1)
+        for k in range(ctx_count)
+    ]
+    first_grad = blocks[0] + sum(
+        swap(blocks[k].astype(BF16), "context", k).astype(F32) for k in range(1, ctx_count)
+    )
+
+    def to_positions(value):
+        parts = [value] + [swap(value, "context", k) for k in range(1, ctx_count)]
+        return sum(dot_f32("msp,msd->mpd", hot_mine[k], parts[k]) for k in range(ctx_count))
+
+    rows_mine = act.astype(F32)
+    inverse_mine = lax.rsqrt(jnp.mean(rows_mine * rows_mine, axis=-1, keepdims=True) + epsilon)
+    rows_back, _ = norm_pull(rows_mine, inverse_mine, gain_one, first_grad)
+    grad_input = (to_positions(hidden_low) + rows_back).astype(BF16)[:, None]
+    output = to_positions(final).astype(BF16)[:, None]
+
+    small = jnp.concatenate([router_total, second_total[:, None], first_total[:, None]], axis=1)
+    small = jnp.pad(small, ((0, 0), (0, 128 - small.shape[1]))).astype(BF16)
+    grad_query, grad_key, grad_value, grad_out, small_sum, diag_all = reduce_dense(
+        qkv_total.astype(BF16), out_total.astype(BF16), small, diagonals, own_width
+    )
+    diag_all = diag_all.reshape((head_count, -1))
+    offsets = jnp.concatenate([diag_all[:, :1], diag_all[:, : seq : -1]], axis=1)
+    grad_table = jnp.einsum(
+        "hs,sb->bh", offsets, bucket_hot.astype(F32), precision=lax.Precision.HIGHEST
+    )
+    return (
+        output,
+        grad_input,
+        grad_query,
+        grad_key,
+        grad_value,
+        grad_out,
+        small_sum[:, :experts],
+        small_sum[:, experts + 1],
+        small_sum[:, experts],
+        grad_table,
+        grad_gate[None],
+        grad_up[None],
+        grad_down[None],
+    )
+
+
+def body(*arguments):
+    counts = tuple(lax.axis_size(name) for name in ALL)
+    activations, w_query, bias_table, w_gate = (arguments[i] for i in (0, 6, 13, 14))
+    own_width = activations.shape[3] // counts[1]
+    fits = (
+        counts == (4, 2, 4)
+        and w_gate.shape[0] == 1
+        and w_query.shape[0] % 16 == 0
+        and own_width % 128 == 0
+        and bias_table.shape[1] % counts[1] == 0
+        and arguments[4].shape[3] == 2
+    )
+    return (tuned_body if fits else plain_body)(*arguments)
+
+
 def solution(mesh):
     tokens = P(None, ("dp", "experts"), "context", None)
     sequences = P(None, ("dp", "experts"))

time: 568 us -> 486 us (0.86)
  Pallas kernels: 83.5 us -> 215 us
  waiting for transfers between devices: 192 us -> 75.4 us
  starting transfers between devices: 93.2 us -> 33.3 us
  local copies, waits for them, and re-layouts: 59.6 us -> 33.7 us
  between operations: 15.8 us -> 1.77 us
    pallas_call x1, Pallas kernels: 7.99 us -> 143 us  [front(): pl.pallas_call(functools.partial(front_kernel, sizes), out_shape=tuple((j...]
    ppermute x37 -> x15, waiting for transfers between devices: 130 us -> 32.4 us  [swap(): return lax.ppermute(value, axis, [(i, i ^ offset) for i in range(size)])]
    ppermute x37 -> x15, starting transfers between devices: 70.5 us -> 21 us  [swap(): return lax.ppermute(value, axis, [(i, i ^ offset) for i in range(size)])]
    ppermute x15 -> x11, waiting for transfers between devices: 62.3 us -> 43 us  [the longest x4 24 us: tuned_body(): arrived = lax.ppermute(piece, ALL, [(b, a) for a, b in pairs])]
    unnamed x114 -> x71, local copies, waits for them, and re-layouts: 29.4 us -> 10.6 us
    ppermute x15 -> x11, starting transfers between devices: 22.7 us -> 12.3 us  [the longest x7 6.8 us: tuned_body(): block = lax.ppermute(block, ALL, pairs)]
    dynamic_update_slice x4 -> x0, local copies, waits for them, and re-layouts: 8.09 us -> none  [body(): down_w = lax.dynamic_update_slice(down_w, piece, (place, 0))]
    dynamic_slice x1 -> x3, local copies, waits for them, and re-layouts: 0.71 us -> 8.35 us  [the longest x1 4.78 us: tuned_body(): lax.dynamic_slice_in_dim(gate_up_total, (plane_index ^ j) * (width // pla...]
  transfers between devices with their start and end apart: 54 -> 26, of which waited for: 20 -> 7; matrix products, arithmetic and copies ran while one was open for 20% -> 19% of each run, Pallas kernels for 15% -> 15%
where the time goes in v2:
time: 486 us; the launch traced here: 477 us
  Pallas kernels  215 us (44%)
  matrix products  90 us (19%)
  waiting for transfers between devices  75.4 us (16%)
  local copies, waits for them, and re-layouts  33.7 us (7%)
  starting transfers between devices  33.3 us (7%)
  other arithmetic  27.5 us (6%)
    pallas_call x1, Pallas kernels, front(): pl.pallas_call(functools.partial(front_kernel, sizes), out_shape=tuple((j...  143 us
    dot_general x23, matrix products, dot_f32(): return jnp.einsum(spec, left, right, preferred_element_type=F32)  89.2 us
    pallas_call x1, Pallas kernels, reduce_dense(): pl.pallas_call(functools.partial(reduce_kernel, own_width), out_shape=tup...  57.4 us
    ppermute x15, waiting for transfers between devices, swap(): return lax.ppermute(value, axis, [(i, i ^ offset) for i in range(size)])  32.4 us
    ppermute x4, waiting for transfers between devices, tuned_body(): arrived = lax.ppermute(piece, ALL, [(b, a) for a, b in pairs])  24 us
    ppermute x15, starting transfers between devices, swap(): return lax.ppermute(value, axis, [(i, i ^ offset) for i in range(size)])  21 us
    ppermute x7, waiting for transfers between devices, tuned_body(): block = lax.ppermute(block, ALL, pairs)  19 us
    pallas_call x1, Pallas kernels, attend_back(): pl.pallas_call(functools.partial(attend_back_kernel, heads, head_size), g...  15.1 us
  transfers between devices with their start and end apart: 26, of which 7 were waited for; matrix products, arithmetic and copies ran while one was open for 19% of the time, Pallas kernels for 15%

profile of v2, /device:TPU:0, one launch (start us, length us, event | category | flops | bytes accessed | tf_op | source)
XLA Modules:
  0.0 476.8 jit_solution(3919971598704120729)
XLA Ops:
  7.7 142.7 %shard_map.264 = (bf16[2,2,2,4,32,1664]{5,4,3,2,1,0:T(8,128)(2,1)}, bf16[2,2,2,4,32,1024]{5,4,3,2,1,0:T(8,128)(2,1)}, bf16[2,256,1024]{2,1,0:T(8,128)(2,1)}, bf1...) custom-call(bf16[2,128,1024]{2,1,0:T(8,128)(2,1)} %bitcast.150, ...), custom_call_target="tpu_custom_call" | custom-call | tf_op jit(solution)/shard_map/pallas_call | solution.py:1279
  153.8 13.1 %fusion.86 = f32[1280,2816]{1,0:T(8,128)} fusion(bf16[1280,1024]{1,0:T(8,128)(2,1)S(1)} %bitcast.198, bf16[1024,2816]{1,0:T(8,128)(2,1)} %bitcast.194), kind=kOutput, calls=%fused_computation.186 | convolution fusion | flops 7381975040 | bytes 22806528 | tf_op jit(solution)/shard_map/rd,df->rf/dot_general | solution.py:18
  166.9 13.0 %multiply_convert_fusion.1 = (bf16[1280,1408]{1,0:T(8,128)(2,1)S(1)}, bf16[1280,1408]{1,0:T(8,128)(2,1)}, bf16[1280,1408]{1,0:T(8,128)(2,1)}) fusion(f32[1280,2816]{1,0:T(8,128)} %fusion.86, bf16[1280,1024]{1,0:T(8,128)(2,1)S(1)} %bitcast.155, bf16[1408,1024]{1,0:T(8,128)(2,1)S(1)} %bitcast.196), kind=kOutput, calls=%fused_computation.3 | convolution fusion | flops 3734241280 | bytes 30736384 | tf_op jit(solution)/shard_map/rd,fd->rf/dot_general | solution.py:18
  181.9 12.0 %convolution_convert_fusion = bf16[1024,2816]{1,0:T(8,128)(2,1)} fusion(bf16[1280,1024]{1,0:T(8,128)(2,1)S(1)} %bitcast.199, bf16[1280,1408]{1,0:T(8,128)(2,1)} %get-tuple-element.130, bf16[1280,1408]{1,0:T(8,128)(2,1)S(1)} %get-tuple-element.129), kind=kOutput, calls=%fused_computation.8 | convolution fusion | flops 7399276544 | bytes 15597568 | tf_op jit(solution)/shard_map/rd,rf->df/dot_general | solution.py:18
  193.9 4.8 %constant_dynamic-slice_fusion.6 = (bf16[128,2816]{1,0:T(8,128)(2,1)}, bf16[128,2816]{1,0:T(8,128)(2,1)}, bf16[128,2816]{1,0:T(8,128)(2,1)}, bf16[128,2816]{1,0:...) fusion(bf16[1024,2816]{1,0:T(8,128)(2,1)} %convolution_convert_fusion, ...), kind=kLoop, calls=%fused_computation.144 | loop fusion | bytes 10092572 | tf_op jit(solution)/shard_map/dynamic_slice | solution.py:1426
  202.8 13.1 %fusion.2 = f32[1280,1024]{1,0:T(8,128)} fusion(bf16[1024,2816]{1,0:T(8,128)(2,1)} %bitcast.195, bf16[1280,1408]{1,0:T(8,128)(2,1)} %get-tuple-element.130, bf16[1280,1408]{1,0:T(8,128)(2,1)} %copy-done.27), kind=kOutput, calls=%fused_computation.12 | convolution fusion | flops 7396392960 | bytes 18219008 | tf_op jit(solution)/shard_map/rf,df->rd/dot_general | solution.py:18
  216.1 3.9 fusion.1
  223.1 7.4 %convolution_convert_fusion.1 = bf16[1408,1024]{1,0:T(8,128)(2,1)} fusion(bf16[1280,1408]{1,0:T(8,128)(2,1)} %get-tuple-element.131, bf16[1280,1024]{1,0:T(8,128)(2,1)S(1)} %copy-done.13), kind=kOutput, calls=%fused_computation.14 | convolution fusion | flops 3692429312 | bytes 9109504 | tf_op jit(solution)/shard_map/rf,rd->fd/dot_general | solution.py:18
  230.5 3.6 constant_dynamic-slice_fusion.3
  234.1 8.0 %fusion.87 = f32[1280,1024]{1,0:T(8,128)} fusion(bf16[1280,1408]{1,0:T(8,128)(2,1)} %get-tuple-element.131, bf16[1408,1024]{1,0:T(8,128)(2,1)S(1)} %bitcast.197), kind=kOutput, calls=%fused_computation.187 | convolution fusion | flops 3690987520 | bytes 11730944 | tf_op jit(solution)/shard_map/rf,fd->rd/dot_general | solution.py:18
  246.5 3.0 slice.275
  249.5 3.0 slice.274
  257.9 3.5 collective-permute-done.20
  261.6 15.5 %collective-permute-done.21 = bf16[128,2816]{1,0:T(8,128)(2,1)} collective-permute-done((bf16[128,2816]{1,0:T(8,128)(2,1)}, bf16[128,2816]{1,0:T(8,128)(2,1)}, u32[]{:S(2)}, u32[]{:S(2)}) %collective-permute-start.21) | collective-permute-done | bytes 720928 | tf_op jit(solution)/shard_map/ppermute | solution.py:1439
  277.1 3.2 broadcast_select_fusion.1
  283.9 7.6 %collective-permute-done.23 = bf16[352,1024]{1,0:T(8,128)(2,1)S(1)} collective-permute-done((bf16[352,1024]{1,0:T(8,128)(2,1)}, bf16[352,1024]{1,0:T(8,128)(2,1)S(1)}, u32[]{:S(2)}, u32[]{:S(2)}) %collective-permute-start.23) | collective-permute-done | bytes 720928 | tf_op jit(solution)/shard_map/ppermute | solution.py:1451
  291.5 16.4 %collective-permute-done.25 = bf16[352,1024]{1,0:T(8,128)(2,1)S(1)} collective-permute-done((bf16[352,1024]{1,0:T(8,128)(2,1)}, bf16[352,1024]{1,0:T(8,128)(2,1)S(1)}, u32[]{:S(2)}, u32[]{:S(2)}) %collective-permute-start.25) | collective-permute-done | bytes 720928 | tf_op jit(solution)/shard_map/ppermute | solution.py:1451
  312.4 3.3 collective-permute-start.9
  331.1 6.4 %collective-permute-done.6 = bf16[2,80,1024]{2,1,0:T(8,128)(2,1)S(1)} collective-permute-done((bf16[2,80,1024]{2,1,0:T(8,128)(2,1)S(1)}, bf16[2,80,1024]{2,1,0:T(8,128)(2,1)S(1)}, u32[]{:S(2)}, u32[]{:S(2)}) %collective-permute-start.6) | collective-permute-done | bytes 327712 | tf_op jit(solution)/shard_map/ppermute | solution.py:23
  339.4 8.3 %collective-permute-done.7 = bf16[2,80,1024]{2,1,0:T(8,128)(2,1)S(1)} collective-permute-done((bf16[2,80,1024]{2,1,0:T(8,128)(2,1)S(1)}, bf16[2,80,1024]{2,1,0:T(8,128)(2,1)S(1)}, u32[]{:S(2)}, u32[]{:S(2)}) %collective-permute-start.7) | collective-permute-done | bytes 327712 | tf_op jit(solution)/shard_map/ppermute | solution.py:23
  357.8 17.6 %collective-permute-done.2 = bf16[2,80,1024]{2,1,0:T(8,128)(2,1)} collective-permute-done((bf16[2,80,1024]{2,1,0:T(8,128)(2,1)}, bf16[2,80,1024]{2,1,0:T(8,128)(2,1)}, u32[]{:S(2)}, u32[]{:S(2)}) %collective-permute-start.2) | collective-permute-done | bytes 327712 | tf_op jit(solution)/shard_map/ppermute | solution.py:23
  382.5 15.1 %shard_map.265 = (bf16[2,256,1536]{2,1,0:T(8,128)(2,1)S(1)}, f32[8,512]{1,0:T(8,128)S(1)}) custom-call(s32[2]{0:T(128)S(1)} %bitcast.146, f32[8,512]{1,0:T(8,128)S(1)} %copy-done.4, bf16[2,256,1536]{2,1,0:T(8,128)(2,1)S(1)} %copy-done.3, bf16[2,256,512]{2,1,0:T(8,128)(2,1)S(1)} %fusion.15.grad_ref), custom_call_target="tpu_custom_call" | custom-call | tf_op jit(solution)/shard_map/pallas_call | solution.py:148
  399.4 3.5 bitcast_convert_fusion
  406.9 57.4 %shard_map.266 = (f32[32,1024]{1,0:T(8,128)S(1)}, f32[32,1024]{1,0:T(8,128)S(1)}, f32[32,1024]{1,0:T(8,128)S(1)}, f32[32,1024]{1,0:T(8,128)S(1)}, f32[32,128]{1,0:T(8,128)S(1)}, /*index=5*/f32[2,8,512]{2,1,0:T(8,128)S(1)}) custom-call(bf16[2,2,256,1536]{3,2,1,0:T(8,128)(2,1)S(1)} %bitcast.139, bf16[2,2,256,1024]{3,2,1,0:T(8,128)(2,1)S(1)} %bitcast.138, ...), custom_call_target="tpu_custom_call" | custom-call | tf_op jit(solution)/shard_map/pallas_call | solution.py:366
  (204 shorter events, 89.8 us)
Async XLA Ops:
  198.7 43.4 %collective-permute-start.15 = (bf16[128,2816]{1,0:T(8,128)(2,1)}, bf16[128,2816]{1,0:T(8,128)(2,1)S(1)}, u32[]{:S(2)}, u32[]{:S(2)}) collective-permute-start(bf16[128,2816]{1,0:T(8,128)(2,1)} %get-tuple-element.140), channel_id=1, source_target_pairs={{0,8},{1,9},{2,10},{3,11},{4,12},{5,13},{6,14},{7,15},{8,0},{9,1},... | collective-permute-start | bytes 2162696 | tf_op jit(solution)/shard_map/ppermute | solution.py:1439
  199.2 44.4 %collective-permute-start.16 = (bf16[128,2816]{1,0:T(8,128)(2,1)}, bf16[128,2816]{1,0:T(8,128)(2,1)}, u32[]{:S(2)}, u32[]{:S(2)}) collective-permute-start(bf16[128,2816]{1,0:T(8,128)(2,1)} %get-tuple-element.139), channel_id=1, source_target_pairs={{0,12},{1,13},{2,14},{3,15},{4,8},{5,9},{6,10},{7,11},{8,4},{9,5},... | collective-permute-start | bytes 2162696 | tf_op jit(solution)/shard_map/ppermute | solution.py:1439
  199.4 53.2 %collective-permute-start.17 = (bf16[128,2816]{1,0:T(8,128)(2,1)}, bf16[128,2816]{1,0:T(8,128)(2,1)}, u32[]{:S(2)}, u32[]{:S(2)}) collective-permute-start(bf16[128,2816]{1,0:T(8,128)(2,1)} %get-tuple-element.138), channel_id=1, source_target_pairs={{0,24},{1,25},{2,26},{3,27},{4,28},{5,29},{6,30},{7,31},{8,16},{9,... | collective-permute-start | bytes 2162696 | tf_op jit(solution)/shard_map/ppermute | solution.py:1439
  200.9 53.4 %collective-permute-start.18 = (bf16[128,2816]{1,0:T(8,128)(2,1)}, bf16[128,2816]{1,0:T(8,128)(2,1)}, u32[]{:S(2)}, u32[]{:S(2)}) collective-permute-start(bf16[128,2816]{1,0:T(8,128)(2,1)} %get-tuple-element.137), channel_id=1, source_target_pairs={{0,28},{1,29},{2,30},{3,31},{4,24},{5,25},{6,26},{7,27},{8,20},{9,... | collective-permute-start | bytes 2162696 | tf_op jit(solution)/shard_map/ppermute | solution.py:1439
  202.0 55.0 %collective-permute-start.19 = (bf16[128,2816]{1,0:T(8,128)(2,1)}, bf16[128,2816]{1,0:T(8,128)(2,1)}, u32[]{:S(2)}, u32[]{:S(2)}) collective-permute-start(bf16[128,2816]{1,0:T(8,128)(2,1)} %get-tuple-element.134), channel_id=1, source_target_pairs={{0,4},{1,5},{2,6},{3,7},{4,0},{5,1},{6,2},{7,3},{8,12},{9,13},{10,... | collective-permute-start | bytes 2162696 | tf_op jit(solution)/shard_map/ppermute | solution.py:1439
  242.1 19.3 %collective-permute-start.20 = (bf16[128,2816]{1,0:T(8,128)(2,1)}, bf16[128,2816]{1,0:T(8,128)(2,1)}, u32[]{:S(2)}, u32[]{:S(2)}) collective-permute-start(bf16[128,2816]{1,0:T(8,128)(2,1)} %get-tuple-element.136), channel_id=1, source_target_pairs={{0,16},{1,17},{2,18},{3,19},{4,20},{5,21},{6,22},{7,23},{8,24},{9,... | collective-permute-start | bytes 2162696 | tf_op jit(solution)/shard_map/ppermute | solution.py:1439
  243.5 33.6 %collective-permute-start.21 = (bf16[128,2816]{1,0:T(8,128)(2,1)}, bf16[128,2816]{1,0:T(8,128)(2,1)}, u32[]{:S(2)}, u32[]{:S(2)}) collective-permute-start(bf16[128,2816]{1,0:T(8,128)(2,1)} %get-tuple-element.135), channel_id=1, source_target_pairs={{0,20},{1,21},{2,22},{3,23},{4,16},{5,17},{6,18},{7,19},{8,28},{9,... | collective-permute-start | bytes 2162696 | tf_op jit(solution)/shard_map/ppermute | solution.py:1439
  252.6 29.1 %collective-permute-start.22 = (bf16[352,1024]{1,0:T(8,128)(2,1)}, bf16[352,1024]{1,0:T(8,128)(2,1)S(1)}, u32[]{:S(2)}, u32[]{:S(2)}) collective-permute-start(bf16[352,1024]{1,0:T(8,128)(2,1)} %get-tuple-element.141), channel_id=1, source_target_pairs={{0,0},{1,1},{2,2},{3,3},{4,4},{5,5},{6,6},{7,7},{16,8},{17,9},{18,... | collective-permute-start | bytes 2162696 | tf_op jit(solution)/shard_map/ppermute | solution.py:1451
  254.3 37.1 %collective-permute-start.23 = (bf16[352,1024]{1,0:T(8,128)(2,1)}, bf16[352,1024]{1,0:T(8,128)(2,1)S(1)}, u32[]{:S(2)}, u32[]{:S(2)}) collective-permute-start(bf16[352,1024]{1,0:T(8,128)(2,1)} %get-tuple-element.144), channel_id=1, source_target_pairs={{16,0},{17,1},{18,2},{19,3},{20,4},{21,5},{22,6},{23,7},{0,8},{1,9... | collective-permute-start | bytes 2162696 | tf_op jit(solution)/shard_map/ppermute | solution.py:1451
  257.0 34.4 %collective-permute-start.24 = (bf16[352,1024]{1,0:T(8,128)(2,1)}, bf16[352,1024]{1,0:T(8,128)(2,1)S(1)}, u32[]{:S(2)}, u32[]{:S(2)}) collective-permute-start(bf16[352,1024]{1,0:T(8,128)(2,1)} %get-tuple-element.143), channel_id=1, source_target_pairs={{4,0},{5,1},{6,2},{7,3},{0,4},{1,5},{2,6},{3,7},{20,8},{21,9},{22,... | collective-permute-start | bytes 2162696 | tf_op jit(solution)/shard_map/ppermute | solution.py:1451
  261.4 46.5 %collective-permute-start.25 = (bf16[352,1024]{1,0:T(8,128)(2,1)}, bf16[352,1024]{1,0:T(8,128)(2,1)S(1)}, u32[]{:S(2)}, u32[]{:S(2)}) collective-permute-start(bf16[352,1024]{1,0:T(8,128)(2,1)} %get-tuple-element.142), channel_id=1, source_target_pairs={{20,0},{21,1},{22,2},{23,3},{16,4},{17,5},{18,6},{19,7},{4,8},{5,9... | collective-permute-start | bytes 2162696 | tf_op jit(solution)/shard_map/ppermute | solution.py:1451
  277.1 33.5 %collective-permute-start = (bf16[640,1024]{1,0:T(8,128)(2,1)}, bf16[640,1024]{1,0:T(8,128)(2,1)S(1)}, u32[]{:S(2)}, u32[]{:S(2)}) collective-permute-start(bf16[640,1024]{1,0:T(8,128)(2,1)} %slice.275), channel_id=1, source_target_pairs={{0,8},{8,0},{16,24},{24,16},{1,9},{9,1},{17,25},{25,17},{2,10},{10... | collective-permute-start | bytes 3932168 | tf_op jit(solution)/shard_map/ppermute | solution.py:23
  281.7 36.5 %collective-permute-start.5 = (bf16[640,1024]{1,0:T(8,128)(2,1)}, bf16[640,1024]{1,0:T(8,128)(2,1)}, u32[]{:S(2)}, u32[]{:S(2)}) collective-permute-start(bf16[640,1024]{1,0:T(8,128)(2,1)} %slice.274), channel_id=1, source_target_pairs={{0,8},{8,0},{16,24},{24,16},{1,9},{9,1},{17,25},{25,17},{2,10},{10... | collective-permute-start | bytes 3932168 | tf_op jit(solution)/shard_map/ppermute | solution.py:23
  312.4 12.4 %collective-permute-start.9 = (f32[2,80]{1,0:T(2,128)S(1)}, f32[2,80]{1,0:T(2,128)S(1)}, u32[]{:S(2)}, u32[]{:S(2)}) collective-permute-start(f32[2,80]{1,0:T(2,128)S(1)} %squeeze.70), channel_id=1, source_target_pairs={{0,1},{1,0},{2,3},{3,2},{4,5},{5,4},{6,7},{7,6},{8,9},{9,8},{10,11... | collective-permute-start | bytes 1928 | tf_op jit(solution)/shard_map/ppermute | solution.py:23
  320.9 16.6 %collective-permute-start.6 = (bf16[2,80,1024]{2,1,0:T(8,128)(2,1)S(1)}, bf16[2,80,1024]{2,1,0:T(8,128)(2,1)S(1)}, u32[]{:S(2)}, u32[]{:S(2)}) collective-permute-start(bf16[2,80,1024]{2,1,0:T(8,128)(2,1)S(1)} %bitcast.167), channel_id=1, source_target_pairs={{0,1},{1,0},{2,3},{3,2},{4,5},{5,4},{6,7},{7,6},{8,9},{9,8},{10,11... | collective-permute-start | bytes 983048 | tf_op jit(solution)/shard_map/ppermute | solution.py:23
  322.1 25.6 %collective-permute-start.7 = (bf16[2,80,1024]{2,1,0:T(8,128)(2,1)S(1)}, bf16[2,80,1024]{2,1,0:T(8,128)(2,1)S(1)}, u32[]{:S(2)}, u32[]{:S(2)}) collective-permute-start(bf16[2,80,1024]{2,1,0:T(8,128)(2,1)S(1)} %bitcast.165), channel_id=1, source_target_pairs={{0,2},{1,3},{2,0},{3,1},{4,6},{5,7},{6,4},{7,5},{8,10},{9,11},{10,... | collective-permute-start | bytes 983048 | tf_op jit(solution)/shard_map/ppermute | solution.py:23
  324.8 22.9 %collective-permute-start.8 = (bf16[2,80,1024]{2,1,0:T(8,128)(2,1)S(1)}, bf16[2,80,1024]{2,1,0:T(8,128)(2,1)}, u32[]{:S(2)}, u32[]{:S(2)}) collective-permute-start(bf16[2,80,1024]{2,1,0:T(8,128)(2,1)S(1)} %bitcast.163), channel_id=1, source_target_pairs={{0,3},{1,2},{2,1},{3,0},{4,7},{5,6},{6,5},{7,4},{8,11},{9,10},{10,... | collective-permute-start | bytes 983048 | tf_op jit(solution)/shard_map/ppermute | solution.py:23
  326.4 31.4 %collective-permute-start.1 = (bf16[2,80,1024]{2,1,0:T(8,128)(2,1)}, bf16[2,80,1024]{2,1,0:T(8,128)(2,1)}, u32[]{:S(2)}, u32[]{:S(2)}) collective-permute-start(bf16[2,80,1024]{2,1,0:T(8,128)(2,1)} %bitcast.17), channel_id=1, source_target_pairs={{0,1},{1,0},{2,3},{3,2},{4,5},{5,4},{6,7},{7,6},{8,9},{9,8},{10,11... | collective-permute-start | bytes 983048 | tf_op jit(solution)/shard_map/ppermute | solution.py:23
  326.7 48.8 %collective-permute-start.2 = (bf16[2,80,1024]{2,1,0:T(8,128)(2,1)}, bf16[2,80,1024]{2,1,0:T(8,128)(2,1)}, u32[]{:S(2)}, u32[]{:S(2)}) collective-permute-start(bf16[2,80,1024]{2,1,0:T(8,128)(2,1)} %bitcast.19), channel_id=1, source_target_pairs={{0,2},{1,3},{2,0},{3,1},{4,6},{5,7},{6,4},{7,5},{8,10},{9,11},{10,... | collective-permute-start | bytes 983048 | tf_op jit(solution)/shard_map/ppermute | solution.py:23
  337.5 37.9 %collective-permute-start.3 = (bf16[2,80,1024]{2,1,0:T(8,128)(2,1)}, bf16[2,80,1024]{2,1,0:T(8,128)(2,1)S(1)}, u32[]{:S(2)}, u32[]{:S(2)}) collective-permute-start(bf16[2,80,1024]{2,1,0:T(8,128)(2,1)} %bitcast.21), channel_id=1, source_target_pairs={{0,3},{1,2},{2,1},{3,0},{4,7},{5,6},{6,5},{7,4},{8,11},{9,10},{10,... | collective-permute-start | bytes 983048 | tf_op jit(solution)/shard_map/ppermute | solution.py:23
  352.5 29.7 %collective-permute-start.13 = (bf16[2,128,512]{2,1,0:T(8,128)(2,1)S(1)}, bf16[2,128,512]{2,1,0:T(8,128)(2,1)S(1)}, u32[]{:S(2)}, u32[]{:S(2)}) collective-permute-start(bf16[2,128,512]{2,1,0:T(8,128)(2,1)S(1)} %broadcast_select_fusion.2), channel_id=1, source_target_pairs={{0,4},{4,0},{1,5},{5,1},{2,6},{6,2},{3,7},{7,3},{8,12},{12,8},{9,1... | collective-permute-start | bytes 786440 | tf_op jit(solution)/shard_map/ppermute | solution.py:23
  353.1 118.0 %collective-permute-start.12 = (bf16[2,128,1024]{2,1,0:T(8,128)(2,1)}, bf16[2,128,1024]{2,1,0:T(8,128)(2,1)}, u32[]{:S(2)}, u32[]{:S(2)}) collective-permute-start(bf16[2,128,1024]{2,1,0:T(8,128)(2,1)} %get-tuple-element.121), channel_id=1, source_target_pairs={{0,4},{4,0},{1,5},{5,1},{2,6},{6,2},{3,7},{7,3},{8,12},{12,8},{9,1... | collective-permute-start | bytes 1572872 | tf_op jit(solution)/shard_map/ppermute | solution.py:23
  378.6 88.2 %collective-permute-start.4 = (bf16[2,128,1024]{2,1,0:T(8,128)(2,1)}, bf16[2,128,1024]{2,1,0:T(8,128)(2,1)}, u32[]{:S(2)}, u32[]{:S(2)}) collective-permute-start(bf16[2,128,1024]{2,1,0:T(8,128)(2,1)} %fusion.16), channel_id=1, source_target_pairs={{0,4},{4,0},{1,5},{5,1},{2,6},{6,2},{3,7},{7,3},{8,12},{12,8},{9,1... | collective-permute-start | bytes 1572872 | tf_op jit(solution)/shard_map/ppermute | solution.py:23
  403.8 65.5 %collective-permute-start.14 = (bf16[2,128,1024]{2,1,0:T(8,128)(2,1)}, bf16[2,128,1024]{2,1,0:T(8,128)(2,1)}, u32[]{:S(2)}, u32[]{:S(2)}) collective-permute-start(bf16[2,128,1024]{2,1,0:T(8,128)(2,1)} %dynamic-slice_convert_fusion), channel_id=1, source_target_pairs={{0,4},{4,0},{1,5},{5,1},{2,6},{6,2},{3,7},{7,3},{8,12},{12,8},{9,1... | collective-permute-start | bytes 1572872 | tf_op jit(solution)/shard_map/ppermute | solution.py:23
  (32 other events, 281.1 us)
